TPU v7x, 128 devices: a whole 4x4x4 slice. The times are simulated.
128 devices in a mesh: blk: 16 (over z, y), group: 8 (over x, core).
Axes of the slice: x: 4, y: 4, z: 4, core: 2. Of those that a mesh axis runs over, the one named last changes fastest.
Arguments:
- embeddings: bfloat16 [16, 8, 8, 128, 768], P('blk', 'group'), may hold values from -6 to 6
- cluster_ids: int32 [16, 8, 8, 128], P('blk', 'group'), may hold values from 0 to 1055, as said below
- orders: int32 [16, 8, 8, 128], P('blk', 'group'), may hold values from 0 to 131071, as said below
Outputs:
- nearest: float32 [16, 8, 8, 128], P('blk', 'group')
Inputs may be any that keep to these rules, and one draw needn't show every extreme that they name: `cluster_ids`: points with equal cluster ids have the same index along the third dimension; the ids under 8 * 4 at third index g are g * 4 to g * 4 + 3 and may occur at every index of the first dimension, larger ids only at one. In each block of 128 points along the last dimension, every id under 8 * 4 occurs at most 32 times, and in every block some id occurs exactly 32 times. `orders`: all values are distinct.
All inputs are finite; a program needn't handle non-finite values.
Results may differ from a plain program's by a relative error of at most 0.0011.
Values may be sent and summed in bfloat16 or wider, within the bound.
A program may use at most 128 MiB of HBM per device.

v0:
```python
import jax
import jax.numpy as jnp
from jax import lax
from jax.sharding import PartitionSpec as P


def block_scores(query, keys):
    return lax.dot_general(
        query, keys, (((1,), (1,)), ((), ())), preferred_element_type=jnp.float32
    )


def shards(embeddings, cluster_ids, orders):
    owned_rows, owned_ids, owned_orders = (
        lax.all_to_all(embeddings, "group", split_axis=2, concat_axis=1, tiled=True),
        lax.all_to_all(cluster_ids, "group", split_axis=2, concat_axis=1, tiled=True),
        lax.all_to_all(orders, "group", split_axis=2, concat_axis=1, tiled=True),
    )
    width = owned_rows.shape[-1]
    values = owned_rows.reshape(-1, width).astype(jnp.float32)
    total = jnp.sum(values * values, axis=1, keepdims=True)
    unit = (values * lax.rsqrt(total + 1e-06)).astype(jnp.bfloat16)
    ident = owned_ids.reshape(-1)
    place = owned_orders.reshape(-1)
    count = unit.shape[0]
    floor_row = jnp.full((count,), -1.0, jnp.float32)
    best = floor_row
    keys = lax.all_gather(unit, "blk", axis=0, tiled=True)
    key_ids = lax.all_gather(ident, "blk", axis=0, tiled=True)
    key_orders = lax.all_gather(place, "blk", axis=0, tiled=True)
    blocks = keys.shape[0] // count

    def inner(carry, item):
        block_keys, block_ids, block_orders = item
        scores = block_scores(unit, block_keys)
        valid = (ident[:, None] == block_ids[None, :]) & (block_orders[None, :] < place[:, None])
        return (jnp.maximum(carry, jnp.max(jnp.where(valid, scores, -1.0), axis=1)), None)

    best, _ = lax.scan(
        inner,
        best,
        (
            keys.reshape(blocks, count, width),
            key_ids.reshape(blocks, count),
            key_orders.reshape(blocks, count),
        ),
    )
    shaped = best.reshape(owned_ids.shape)
    return lax.all_to_all(shaped, "group", split_axis=1, concat_axis=2, tiled=True)


def solution(mesh):
    in_specs = (
        P("blk", "group", None, None, None),
        P("blk", "group", None, None),
        P("blk", "group", None, None),
    )
    out_specs = P("blk", "group", None, None)
    return jax.shard_map(shards, mesh=mesh, in_specs=in_specs, out_specs=out_specs, check_vma=False)
```

profile of v0, /device:TPU:1, one launch (start us, length us, event | category | flops | bytes accessed | tf_op | source)
XLA Modules:
  0.0 270.1 jit_solution(16564445411537500512)
XLA Ops:
  6.5 0.0 all-gather.2.cloned.1.call-start
  6.5 26.6 %all_to_all.45 = bf16[1,1,8,128,768]{4,3,1,0,2:T(8,128)(2,1)S(1)} all-to-all(bf16[1,1,8,128,768]{4,3,1,0,2:T(8,128)(2,1)} %bitcast.46), channel_id=1, replica_groups=mesh['blk'=16,'group'=8] {'group'}, dimensions={2} | all-to-all | bytes 3145728 | tf_op jit(solution)/shard_map/all_to_all | solution.py:15
  33.1 0.4 multiply_reduce_fusion
  33.5 1.6 fusion.4
  35.0 0.0 all-gather.2.cloned.1.call-update
  35.1 4.3 %all-to-all-start = ((s32[1,1,8,128]{3,1,0,2:T(1,128)}), s32[1,1,8,128]{3,1,0,2:T(1,128)S(1)}, u32[]{:S(2)}, u32[]{:S(2)}) async-start(s32[1,1,8,128]{3,1,0,2:T(1,128)} %bitcast), calls=%async_computation | async-start | bytes 8192 | tf_op jit(solution)/shard_map/all_to_all | solution.py:16
  39.3 4.5 %all-to-all-done = s32[1,1,8,128]{3,1,0,2:T(1,128)S(1)} async-done(((s32[1,1,8,128]{3,1,0,2:T(1,128)}), s32[1,1,8,128]{3,1,0,2:T(1,128)S(1)}, u32[]{:S(2)}, u32[]{:S(2)}) %all-to-all-start) | async-done | bytes 4128 | tf_op jit(solution)/shard_map/all_to_all | solution.py:16
  43.9 3.9 %all-to-all-start.1 = ((s32[1,1,8,128]{3,1,0,2:T(1,128)}), s32[1,1,8,128]{3,1,0,2:T(1,128)S(1)}, u32[]{:S(2)}, u32[]{:S(2)}) async-start(s32[1,1,8,128]{3,1,0,2:T(1,128)} %bitcast.4), calls=%async_computation.1 | async-start | bytes 8192 | tf_op jit(solution)/shard_map/all_to_all | solution.py:17
  47.8 21.9 %all_gather.9 = s32[16384]{0:T(1024)S(1)} all-gather(s32[1024]{0:T(1024)S(1)} %bitcast.50), channel_id=1, replica_groups=mesh['blk'=16,'group'=8] {'blk'}, dimensions={0}, use_global_device_ids=true | all-gather | bytes 69632 | tf_op jit(solution)/shard_map/all_gather | solution.py:29
  69.7 0.0 all-to-all-done.1
  69.7 18.0 %all_gather.10 = s32[16384]{0:T(1024)S(1)} all-gather(s32[1024]{0:T(1024)S(1)} %bitcast.53), channel_id=1, replica_groups=mesh['blk'=16,'group'=8] {'blk'}, dimensions={0}, use_global_device_ids=true | all-gather | bytes 69632 | tf_op jit(solution)/shard_map/all_gather | solution.py:30
  87.7 103.4 %all-gather.2.cloned.1.call-done = bf16[16384,768]{1,0:T(8,128)(2,1)} async-done(((bf16[1024,768]{1,0:T(8,128)(2,1)}), bf16[16384,768]{1,0:T(8,128)(2,1)}) %all-gather.2.cloned.1.call-update) | async-done | bytes 25165840 | tf_op jit(solution)/shard_map/all_gather | solution.py:28
  191.1 62.1 %while.11 = (s32[]{:T(128)}, f32[1024]{0:T(1024)S(1)}, s32[1,8,1,128]{3,2,1,0:T(1,128)S(1)}, s32[16,1024]{1,0:T(8,128)S(1)}, s32[16,1024]{1,0:T(8,128)S(1)}, /*i...) while((s32[]{:T(128)}, f32[1024]{0:T(1024)S(1)}, ...), condition=%wide.region_3.4_spmd.clone, body=%wide.region_1.3_spmd.clone.sunk | while | flops 1615856640 | bytes 3195007 | solution.py:39
  191.2 3.8 %fusion.11 = f32[1024]{0:T(1024)S(1)} fusion(bf16[1024,768]{1,0:T(8,128)(2,1)} %get-tuple-element.181, s32[1024]{0:T(1024)S(1)} %bitcast.55, s32[1024]{0:T(1024)S(1)} %bitcast.52, s32[1024]{0:T(1024)S(1)} %bitcast.48, s32[1024]{0:T(1024)S(1)} %bitcast.49, bf16[16,1024,768]{2,1,0:T(8,128)(2,1)} %get-tuple-element.180, s32[]{:T(128)S(6)} %copy.11), kind=kOutput, calls=%fused_computation.1.clone.1 | convolution fusion | flops 1615854592 | bytes 3166212 | tf_op jit(solution)/shard_map/while/body/eval_jaxpr/dot_general | solution.py:8
  195.0 3.8 %fusion.11 = f32[1024]{0:T(1024)S(1)} fusion(bf16[1024,768]{1,0:T(8,128)(2,1)} %get-tuple-element.181, s32[1024]{0:T(1024)S(1)} %bitcast.55, s32[1024]{0:T(1024)S(1)} %bitcast.52, s32[1024]{0:T(1024)S(1)} %bitcast.48, s32[1024]{0:T(1024)S(1)} %bitcast.49, bf16[16,1024,768]{2,1,0:T(8,128)(2,1)} %get-tuple-element.180, s32[]{:T(128)S(6)} %copy.11), kind=kOutput, calls=%fused_computation.1.clone.1 | convolution fusion | flops 1615854592 | bytes 3166212 | tf_op jit(solution)/shard_map/while/body/eval_jaxpr/dot_general | solution.py:8
  198.9 3.8 %fusion.11 = f32[1024]{0:T(1024)S(1)} fusion(bf16[1024,768]{1,0:T(8,128)(2,1)} %get-tuple-element.181, s32[1024]{0:T(1024)S(1)} %bitcast.55, s32[1024]{0:T(1024)S(1)} %bitcast.52, s32[1024]{0:T(1024)S(1)} %bitcast.48, s32[1024]{0:T(1024)S(1)} %bitcast.49, bf16[16,1024,768]{2,1,0:T(8,128)(2,1)} %get-tuple-element.180, s32[]{:T(128)S(6)} %copy.11), kind=kOutput, calls=%fused_computation.1.clone.1 | convolution fusion | flops 1615854592 | bytes 3166212 | tf_op jit(solution)/shard_map/while/body/eval_jaxpr/dot_general | solution.py:8
  202.8 3.8 %fusion.11 = f32[1024]{0:T(1024)S(1)} fusion(bf16[1024,768]{1,0:T(8,128)(2,1)} %get-tuple-element.181, s32[1024]{0:T(1024)S(1)} %bitcast.55, s32[1024]{0:T(1024)S(1)} %bitcast.52, s32[1024]{0:T(1024)S(1)} %bitcast.48, s32[1024]{0:T(1024)S(1)} %bitcast.49, bf16[16,1024,768]{2,1,0:T(8,128)(2,1)} %get-tuple-element.180, s32[]{:T(128)S(6)} %copy.11), kind=kOutput, calls=%fused_computation.1.clone.1 | convolution fusion | flops 1615854592 | bytes 3166212 | tf_op jit(solution)/shard_map/while/body/eval_jaxpr/dot_general | solution.py:8
  206.7 3.8 %fusion.11 = f32[1024]{0:T(1024)S(1)} fusion(bf16[1024,768]{1,0:T(8,128)(2,1)} %get-tuple-element.181, s32[1024]{0:T(1024)S(1)} %bitcast.55, s32[1024]{0:T(1024)S(1)} %bitcast.52, s32[1024]{0:T(1024)S(1)} %bitcast.48, s32[1024]{0:T(1024)S(1)} %bitcast.49, bf16[16,1024,768]{2,1,0:T(8,128)(2,1)} %get-tuple-element.180, s32[]{:T(128)S(6)} %copy.11), kind=kOutput, calls=%fused_computation.1.clone.1 | convolution fusion | flops 1615854592 | bytes 3166212 | tf_op jit(solution)/shard_map/while/body/eval_jaxpr/dot_general | solution.py:8
  210.6 3.9 %fusion.11 = f32[1024]{0:T(1024)S(1)} fusion(bf16[1024,768]{1,0:T(8,128)(2,1)} %get-tuple-element.181, s32[1024]{0:T(1024)S(1)} %bitcast.55, s32[1024]{0:T(1024)S(1)} %bitcast.52, s32[1024]{0:T(1024)S(1)} %bitcast.48, s32[1024]{0:T(1024)S(1)} %bitcast.49, bf16[16,1024,768]{2,1,0:T(8,128)(2,1)} %get-tuple-element.180, s32[]{:T(128)S(6)} %copy.11), kind=kOutput, calls=%fused_computation.1.clone.1 | convolution fusion | flops 1615854592 | bytes 3166212 | tf_op jit(solution)/shard_map/while/body/eval_jaxpr/dot_general | solution.py:8
  214.5 3.8 %fusion.11 = f32[1024]{0:T(1024)S(1)} fusion(bf16[1024,768]{1,0:T(8,128)(2,1)} %get-tuple-element.181, s32[1024]{0:T(1024)S(1)} %bitcast.55, s32[1024]{0:T(1024)S(1)} %bitcast.52, s32[1024]{0:T(1024)S(1)} %bitcast.48, s32[1024]{0:T(1024)S(1)} %bitcast.49, bf16[16,1024,768]{2,1,0:T(8,128)(2,1)} %get-tuple-element.180, s32[]{:T(128)S(6)} %copy.11), kind=kOutput, calls=%fused_computation.1.clone.1 | convolution fusion | flops 1615854592 | bytes 3166212 | tf_op jit(solution)/shard_map/while/body/eval_jaxpr/dot_general | solution.py:8
  218.4 3.8 %fusion.11 = f32[1024]{0:T(1024)S(1)} fusion(bf16[1024,768]{1,0:T(8,128)(2,1)} %get-tuple-element.181, s32[1024]{0:T(1024)S(1)} %bitcast.55, s32[1024]{0:T(1024)S(1)} %bitcast.52, s32[1024]{0:T(1024)S(1)} %bitcast.48, s32[1024]{0:T(1024)S(1)} %bitcast.49, bf16[16,1024,768]{2,1,0:T(8,128)(2,1)} %get-tuple-element.180, s32[]{:T(128)S(6)} %copy.11), kind=kOutput, calls=%fused_computation.1.clone.1 | convolution fusion | flops 1615854592 | bytes 3166212 | tf_op jit(solution)/shard_map/while/body/eval_jaxpr/dot_general | solution.py:8
  222.3 3.8 %fusion.11 = f32[1024]{0:T(1024)S(1)} fusion(bf16[1024,768]{1,0:T(8,128)(2,1)} %get-tuple-element.181, s32[1024]{0:T(1024)S(1)} %bitcast.55, s32[1024]{0:T(1024)S(1)} %bitcast.52, s32[1024]{0:T(1024)S(1)} %bitcast.48, s32[1024]{0:T(1024)S(1)} %bitcast.49, bf16[16,1024,768]{2,1,0:T(8,128)(2,1)} %get-tuple-element.180, s32[]{:T(128)S(6)} %copy.11), kind=kOutput, calls=%fused_computation.1.clone.1 | convolution fusion | flops 1615854592 | bytes 3166212 | tf_op jit(solution)/shard_map/while/body/eval_jaxpr/dot_general | solution.py:8
  226.1 3.8 %fusion.11 = f32[1024]{0:T(1024)S(1)} fusion(bf16[1024,768]{1,0:T(8,128)(2,1)} %get-tuple-element.181, s32[1024]{0:T(1024)S(1)} %bitcast.55, s32[1024]{0:T(1024)S(1)} %bitcast.52, s32[1024]{0:T(1024)S(1)} %bitcast.48, s32[1024]{0:T(1024)S(1)} %bitcast.49, bf16[16,1024,768]{2,1,0:T(8,128)(2,1)} %get-tuple-element.180, s32[]{:T(128)S(6)} %copy.11), kind=kOutput, calls=%fused_computation.1.clone.1 | convolution fusion | flops 1615854592 | bytes 3166212 | tf_op jit(solution)/shard_map/while/body/eval_jaxpr/dot_general | solution.py:8
  230.0 3.8 %fusion.11 = f32[1024]{0:T(1024)S(1)} fusion(bf16[1024,768]{1,0:T(8,128)(2,1)} %get-tuple-element.181, s32[1024]{0:T(1024)S(1)} %bitcast.55, s32[1024]{0:T(1024)S(1)} %bitcast.52, s32[1024]{0:T(1024)S(1)} %bitcast.48, s32[1024]{0:T(1024)S(1)} %bitcast.49, bf16[16,1024,768]{2,1,0:T(8,128)(2,1)} %get-tuple-element.180, s32[]{:T(128)S(6)} %copy.11), kind=kOutput, calls=%fused_computation.1.clone.1 | convolution fusion | flops 1615854592 | bytes 3166212 | tf_op jit(solution)/shard_map/while/body/eval_jaxpr/dot_general | solution.py:8
  233.9 3.8 %fusion.11 = f32[1024]{0:T(1024)S(1)} fusion(bf16[1024,768]{1,0:T(8,128)(2,1)} %get-tuple-element.181, s32[1024]{0:T(1024)S(1)} %bitcast.55, s32[1024]{0:T(1024)S(1)} %bitcast.52, s32[1024]{0:T(1024)S(1)} %bitcast.48, s32[1024]{0:T(1024)S(1)} %bitcast.49, bf16[16,1024,768]{2,1,0:T(8,128)(2,1)} %get-tuple-element.180, s32[]{:T(128)S(6)} %copy.11), kind=kOutput, calls=%fused_computation.1.clone.1 | convolution fusion | flops 1615854592 | bytes 3166212 | tf_op jit(solution)/shard_map/while/body/eval_jaxpr/dot_general | solution.py:8
  237.8 3.8 %fusion.11 = f32[1024]{0:T(1024)S(1)} fusion(bf16[1024,768]{1,0:T(8,128)(2,1)} %get-tuple-element.181, s32[1024]{0:T(1024)S(1)} %bitcast.55, s32[1024]{0:T(1024)S(1)} %bitcast.52, s32[1024]{0:T(1024)S(1)} %bitcast.48, s32[1024]{0:T(1024)S(1)} %bitcast.49, bf16[16,1024,768]{2,1,0:T(8,128)(2,1)} %get-tuple-element.180, s32[]{:T(128)S(6)} %copy.11), kind=kOutput, calls=%fused_computation.1.clone.1 | convolution fusion | flops 1615854592 | bytes 3166212 | tf_op jit(solution)/shard_map/while/body/eval_jaxpr/dot_general | solution.py:8
  241.7 3.8 %fusion.11 = f32[1024]{0:T(1024)S(1)} fusion(bf16[1024,768]{1,0:T(8,128)(2,1)} %get-tuple-element.181, s32[1024]{0:T(1024)S(1)} %bitcast.55, s32[1024]{0:T(1024)S(1)} %bitcast.52, s32[1024]{0:T(1024)S(1)} %bitcast.48, s32[1024]{0:T(1024)S(1)} %bitcast.49, bf16[16,1024,768]{2,1,0:T(8,128)(2,1)} %get-tuple-element.180, s32[]{:T(128)S(6)} %copy.11), kind=kOutput, calls=%fused_computation.1.clone.1 | convolution fusion | flops 1615854592 | bytes 3166212 | tf_op jit(solution)/shard_map/while/body/eval_jaxpr/dot_general | solution.py:8
  245.6 3.8 %fusion.11 = f32[1024]{0:T(1024)S(1)} fusion(bf16[1024,768]{1,0:T(8,128)(2,1)} %get-tuple-element.181, s32[1024]{0:T(1024)S(1)} %bitcast.55, s32[1024]{0:T(1024)S(1)} %bitcast.52, s32[1024]{0:T(1024)S(1)} %bitcast.48, s32[1024]{0:T(1024)S(1)} %bitcast.49, bf16[16,1024,768]{2,1,0:T(8,128)(2,1)} %get-tuple-element.180, s32[]{:T(128)S(6)} %copy.11), kind=kOutput, calls=%fused_computation.1.clone.1 | convolution fusion | flops 1615854592 | bytes 3166212 | tf_op jit(solution)/shard_map/while/body/eval_jaxpr/dot_general | solution.py:8
  249.4 3.8 %fusion.11 = f32[1024]{0:T(1024)S(1)} fusion(bf16[1024,768]{1,0:T(8,128)(2,1)} %get-tuple-element.181, s32[1024]{0:T(1024)S(1)} %bitcast.55, s32[1024]{0:T(1024)S(1)} %bitcast.52, s32[1024]{0:T(1024)S(1)} %bitcast.48, s32[1024]{0:T(1024)S(1)} %bitcast.49, bf16[16,1024,768]{2,1,0:T(8,128)(2,1)} %get-tuple-element.180, s32[]{:T(128)S(6)} %copy.11), kind=kOutput, calls=%fused_computation.1.clone.1 | convolution fusion | flops 1615854592 | bytes 3166212 | tf_op jit(solution)/shard_map/while/body/eval_jaxpr/dot_general | solution.py:8
  253.3 9.4 %all_to_all.46 = f32[1,8,1,128]{3,2,0,1:T(1,128)S(1)} all-to-all(f32[1,8,1,128]{3,2,0,1:T(1,128)S(1)} %bitcast.47), channel_id=1, replica_groups=mesh['blk'=16,'group'=8] {'group'}, dimensions={1} | all-to-all | bytes 8192 | tf_op jit(solution)/shard_map/all_to_all | solution.py:49
  262.7 0.6 copy.16
  (36 shorter events, 0.4 us)
Async XLA Ops:
  6.5 184.6 %all-gather.2.cloned.1.call-start = ((), (), s32[]{:S(2)}) async-start(), calls=%async_computation.4 | async-start | bytes 26738688 | tf_op jit(solution)/shard_map/all_gather | solution.py:28
  35.1 8.8 %all-to-all-start = ((s32[1,1,8,128]{3,1,0,2:T(1,128)}), s32[1,1,8,128]{3,1,0,2:T(1,128)S(1)}, u32[]{:S(2)}, u32[]{:S(2)}) async-start(s32[1,1,8,128]{3,1,0,2:T(1,128)} %bitcast), calls=%async_computation | async-start | bytes 8192 | tf_op jit(solution)/shard_map/all_to_all | solution.py:16
  43.9 25.9 %all-to-all-start.1 = ((s32[1,1,8,128]{3,1,0,2:T(1,128)}), s32[1,1,8,128]{3,1,0,2:T(1,128)S(1)}, u32[]{:S(2)}, u32[]{:S(2)}) async-start(s32[1,1,8,128]{3,1,0,2:T(1,128)} %bitcast.4), calls=%async_computation.1 | async-start | bytes 8192 | tf_op jit(solution)/shard_map/all_to_all | solution.py:17
Sparse Core Ops, SparseCore 0:
  35.2 155.8 all-gather.1
where the time goes:
time: 271 us; the launch traced here: 270 us
  waiting for transfers between devices  108 us (40%)
  blocking collectives  75.8 us (28%)
  matrix products  61.2 us (23%)
  between operations  13.4 us (5%)
  starting transfers between devices  8.18 us (3%)
    all_gather x1, waiting for transfers between devices, shards(): keys = lax.all_gather(unit, 'blk', axis=0, tiled=True)  103 us
    dot_general x16, matrix products, block_scores(): lax.dot_general(query, keys, (((1,), (1,)), ((), ())), preferred_element_...  61.2 us
    all_to_all x1, blocking collectives, shards(): lax.all_to_all(embeddings, 'group', split_axis=2, concat_axis=1, tiled=True)  26.6 us
    all_gather x1, blocking collectives, shards(): key_ids = lax.all_gather(ident, 'blk', axis=0, tiled=True)  21.9 us
    all_gather x1, blocking collectives, shards(): key_orders = lax.all_gather(place, 'blk', axis=0, tiled=True)  18 us
    all_to_all x1, blocking collectives, shards(): lax.all_to_all(shaped, 'group', split_axis=1, concat_axis=2, tiled=True)  9.38 us
  transfers between devices with their start and end apart: 3, of which 2 were waited for; matrix products, arithmetic and copies ran while one was open for 0% of the time, Pallas kernels for 0%

commit v1 on v0

v1 whole, which is shorter than its diff:
```python
import functools

import jax
import jax.numpy as jnp
from jax import lax
from jax.experimental import pallas as pl
from jax.experimental.pallas import tpu as pltpu
from jax.sharding import PartitionSpec as P

MESH = pl.DeviceIdType.MESH
F32 = jnp.float32
BF16 = jnp.bfloat16
D = 768
SLOT = 128
CAP = 32
LARGE_IDS = 32.0
NEVER = 1.0e9


def flip(value, bits):
    out = 0
    for shift in (1, 2, 4):
        bit = lax.rem(lax.div(value, shift), 2) + lax.rem(lax.div(bits, shift), 2)
        out = out + shift * lax.rem(bit, 2)
    return out


def iota(shape, dim):
    return lax.broadcasted_iota(jnp.int32, shape, dim)


def to_column(row):
    eye = iota((SLOT, SLOT), 0) == iota((SLOT, SLOT), 1)
    return jnp.sum(jnp.where(eye, jnp.broadcast_to(row, (SLOT, SLOT)), 0.0), axis=1, keepdims=True)


def to_row(column):
    eye = iota((SLOT, SLOT), 0) == iota((SLOT, SLOT), 1)
    return jnp.sum(jnp.where(eye, jnp.broadcast_to(column, (SLOT, SLOT)), 0.0), axis=0, keepdims=True)


def product(query, keys):
    return lax.dot_general(query, keys, (((1,), (1,)), ((), ())), preferred_element_type=F32)


def permutation(ids, group):
    large = ids < LARGE_IDS
    label = jnp.where(large, ids - 4.0 * group.astype(F32), 4.0)
    sub = iota((SLOT, SLOT), 0)
    lane = iota((SLOT, SLOT), 1)
    before = jnp.where((to_column(label) == label) & (sub < lane), 1.0, 0.0)
    rank = jnp.sum(before, axis=0, keepdims=True)
    dest = jnp.where(large, CAP * label + rank, 4096.0)
    subf = sub.astype(F32)
    taken = jnp.where(dest == subf, 1024.0, 0.0) + jnp.where(dest < subf, 1.0, 0.0)
    slot = iota((SLOT, 1), 0).astype(F32)
    free = slot - jnp.sum(taken, axis=1, keepdims=True)
    return jnp.where((dest == subf) | (free == jnp.where(large, -8192.0, rank)), 1.0, 0.0)


def permuted_meta(ids, orders, perm):
    id_high = jnp.floor(ids * (1.0 / 32))
    order_high = jnp.floor(orders * (1.0 / 1024))
    rest = orders - 1024.0 * order_high
    order_mid = jnp.floor(rest * (1.0 / 32))
    at = iota((8, SLOT), 0)
    parts = jnp.zeros((8, SLOT), F32)
    pieces = (id_high, ids - 32.0 * id_high, order_high, order_mid, rest - 32.0 * order_mid)
    for index, piece in enumerate(pieces):
        parts = jnp.where(at == index, jnp.broadcast_to(piece, (8, SLOT)), parts)
    moved = product(parts, perm)
    slot_ids = moved[0:1] * 32.0 + moved[1:2]
    slot_orders = moved[2:3] * 1024.0 + moved[3:4] * 32.0 + moved[4:5]
    large_orders = jnp.where(slot_ids < LARGE_IDS, slot_orders, NEVER)
    out = jnp.where(at == 0, jnp.broadcast_to(slot_ids, (8, SLOT)), jnp.broadcast_to(slot_orders, (8, SLOT)))
    return jnp.where(at == 2, jnp.broadcast_to(large_orders, (8, SLOT)), out)


def kernel(
    emb, ids_ref, orders_ref, out_ref,
    raw, send, recv, meta_send, meta_recv, perms, plane_meta, keys, key_meta, key_orders,
    best, large_in, small_best, final_send, final_recv,
    load_sem, xs, xr, xms, xmr, ps, pr, pms, pmr, fs, fr, fms, fmr, rs, rr, os, orr,
):
    b = lax.axis_index("blk")
    g = lax.axis_index("group")
    z, y = lax.div(b, 4), lax.rem(b, 4)
    x, core = lax.div(g, 2), lax.rem(g, 2)
    half = lax.div(z, 2)
    offset = lax.rem(y - z + 4, 4)
    busy = lax.rem(offset, 2) == 0
    host = lax.div(offset, 2)
    both = busy & (host == core)

    def target(c):
        return 4 * c + lax.rem(2 * core + c, 4)

    def relation(k):
        return lax.rem(3 * k, 8)

    def partner(k):
        return flip(g, relation(k))

    def load(k):
        return pltpu.make_async_copy(emb.at[partner(k)], raw.at[k], load_sem.at[k])

    def load_step(k, carry):
        load(k).start()
        return carry

    lax.fori_loop(0, 8, load_step, 0)

    barrier = pltpu.get_barrier_semaphore()

    def greet_line(k, carry):
        pl.semaphore_signal(barrier, inc=1, device_id=(b, partner(k)), device_id_type=MESH)
        return carry

    lax.fori_loop(1, 8, greet_line, 0)

    def greet_targets(c, carry):
        for h in range(2):
            @pl.when(jnp.logical_not((target(c) == b) & (core == h)))
            def _():
                pl.semaphore_signal(barrier, inc=1, device_id=(target(c), 2 * x + h), device_id_type=MESH)
        return carry

    lax.fori_loop(0, 4, greet_targets, 0)

    @pl.when(busy)
    def _():
        def greet_senders(i, carry):
            @pl.when(jnp.logical_not((i == b) & (host == core)))
            def _():
                pl.semaphore_signal(barrier, inc=1, device_id=(i, 2 * x + host), device_id_type=MESH)
            return carry

        lax.fori_loop(0, 16, greet_senders, 0)

    def prepare(k):
        load(k).wait()
        owner = partner(k)
        ids = ids_ref[pl.ds(owner, 1), :].astype(F32)
        orders = orders_ref[pl.ds(owner, 1), :].astype(F32)
        perm = permutation(ids, owner)
        perms[k] = perm
        values = raw[k].astype(F32)
        total = jnp.sum(values * values, axis=1, keepdims=True)
        unit = (values * lax.rsqrt(total + 1e-06)).astype(BF16)
        rows = jnp.dot(perm.astype(BF16), unit, preferred_element_type=F32).astype(BF16)
        return rows, permuted_meta(ids, orders, perm)

    def x_copies(k):
        to = (b, partner(k))
        return (
            pltpu.make_async_remote_copy(send.at[k], recv.at[k], xs.at[k], xr.at[k], to, MESH),
            pltpu.make_async_remote_copy(meta_send.at[k], meta_recv.at[k], xms.at[k], xmr.at[k], to, MESH),
        )

    def plane_copies(k, c):
        to = (target(c), 2 * x + half)
        rows = pl.ds(pl.multiple_of(c * CAP, CAP), CAP)
        spot = pl.ds(pl.multiple_of(b * CAP, CAP), CAP)
        return (
            pltpu.make_async_remote_copy(
                recv.at[k, rows], keys.at[k, spot], ps.at[k, c], pr.at[k], to, MESH),
            pltpu.make_async_remote_copy(
                plane_meta.at[k], key_meta.at[k, b], pms.at[k, c], pmr.at[k], to, MESH),
            pltpu.make_async_copy(recv.at[k, rows], keys.at[k, spot], pr.at[k]),
            pltpu.make_async_copy(plane_meta.at[k], key_meta.at[k, b], pmr.at[k]),
        )

    def is_self(c):
        return (target(c) == b) & (core == half)

    def send_plane(k):
        plane_meta[k] = meta_recv[k, 2:3, :]

        def piece(c, carry):
            far_rows, far_meta, near_rows, near_meta = plane_copies(k, c)

            @pl.when(jnp.logical_not(is_self(c)))
            def _():
                far_meta.start()
                far_rows.start()

            @pl.when(is_self(c))
            def _():
                near_meta.start()
                near_rows.start()

            return carry

        lax.fori_loop(0, 4, piece, 0)

    def share_copies(k):
        to = (b, 2 * x + 1 - core)
        rows = pl.ds(pl.multiple_of(core * 256, 256), 256)
        sources = pl.ds(pl.multiple_of(core * 8, 8), 8)
        return (
            pltpu.make_async_remote_copy(keys.at[k, rows], keys.at[k, rows], fs.at[k], fr.at[k], to, MESH),
            pltpu.make_async_remote_copy(
                key_meta.at[k, sources], key_meta.at[k, sources], fms.at[k], fmr.at[k], to, MESH),
        )

    def share(k):
        rows = keys.at[k, pl.ds(pl.multiple_of(core * 256, 256), 256)]
        sources = key_meta.at[k, pl.ds(pl.multiple_of(core * 8, 8), 8)]
        pltpu.make_async_copy(sources, sources, pmr.at[k]).wait()
        pltpu.make_async_copy(rows, rows, pr.at[k]).wait()
        for copy in share_copies(k):
            copy.start()

    lane_part = lax.div(iota((1, SLOT), 1), CAP)

    def compare(k):
        for copy in share_copies(k):
            copy.wait_recv()
        for u in range(4):
            merged = jnp.zeros((1, SLOT), F32)
            for j in range(4):
                shift = lax.rem(CAP * (j - z) + SLOT, SLOT)
                merged = jnp.where(lane_part == j, pltpu.roll(key_meta[k, 4 * u + j], shift, 1), merged)
            key_orders[k, u:u + 1, :] = merged
        query = keys[k, pl.ds(pl.multiple_of(core * 256, 256), 256)]
        places = jnp.concatenate(
            [to_column(key_orders[k, pl.ds(2 * core + i, 1), :]) for i in range(2)], axis=0)

        def old(j, found):
            for h in range(2):
                scores = product(query, keys[j, h * 256:(h + 1) * 256])
                for i in range(2):
                    u = 2 * h + i
                    part = scores[:, i * SLOT:(i + 1) * SLOT]
                    earlier = key_orders[j, u:u + 1, :] < places
                    found = jnp.maximum(found, jnp.where(earlier, part, -1.0))
                    other = jnp.max(jnp.where(earlier, -1.0, part), axis=0, keepdims=True)
                    best[u, pl.ds(j, 1), :] = jnp.maximum(best[u, pl.ds(j, 1), :], other)
            return found

        found = lax.fori_loop(0, k, old, jnp.full((256, SLOT), -1.0, F32))
        for h in range(2):
            scores = product(query, keys[k, h * 256:(h + 1) * 256])
            for i in range(2):
                u = 2 * h + i
                earlier = key_orders[k, u:u + 1, :] < places
                found = jnp.maximum(found, jnp.where(earlier, scores[:, i * SLOT:(i + 1) * SLOT], -1.0))
        column = jnp.max(found, axis=1, keepdims=True)
        for i in range(2):
            best[2 * core + i, pl.ds(k, 1), :] = to_row(column[i * SLOT:(i + 1) * SLOT])

    best[...] = jnp.full(best.shape, -1.0, F32)

    rows, meta = prepare(0)
    recv[0] = rows
    meta_recv[0] = meta

    greeted = 15 + jnp.where(busy, 16, 0) - jnp.where(both, 2, 0)
    pl.semaphore_wait(barrier, greeted)
    send_plane(0)

    def outgoing(k, carry):
        rows, meta = prepare(k)
        send[k] = rows
        meta_send[k] = meta
        for copy in x_copies(k):
            copy.start()
        return carry

    lax.fori_loop(1, 8, outgoing, 0)

    def pass_on(k, carry):
        for copy in x_copies(k):
            copy.wait_recv()
        send_plane(k)

        @pl.when(busy)
        def _():
            share(k - 1)

            @pl.when(k >= 2)
            def _():
                compare(k - 2)

        return carry

    lax.fori_loop(1, 8, pass_on, 0)

    def small(q, carry):
        query = jnp.concatenate([recv[2 * q], recv[2 * q + 1]], axis=0)
        labels = jnp.concatenate([to_column(meta_recv[2 * q + i, 0:1, :]) for i in range(2)], axis=0)
        labels = jnp.where(labels < LARGE_IDS, -1.0, labels)
        places = jnp.concatenate([to_column(meta_recv[2 * q + i, 1:2, :]) for i in range(2)], axis=0)

        def pair(j, found):
            scores = product(query, jnp.concatenate([recv[2 * j], recv[2 * j + 1]], axis=0))
            for i in range(2):
                match = (meta_recv[2 * j + i, 0:1, :] == labels) & (meta_recv[2 * j + i, 1:2, :] < places)
                found = jnp.maximum(found, jnp.where(match, scores[:, i * SLOT:(i + 1) * SLOT], -1.0))
            return found

        found = lax.fori_loop(0, 4, pair, jnp.full((256, SLOT), -1.0, F32))
        column = jnp.max(found, axis=1, keepdims=True)
        for i in range(2):
            small_best[pl.ds(2 * q + i, 1), :] = to_row(column[i * SLOT:(i + 1) * SLOT])
        return carry

    lax.fori_loop(0, 4, small, 0)

    def result_copies(i):
        spot = 2 * z + core
        return (
            pltpu.make_async_remote_copy(
                best.at[lax.div(i, 4)], large_in.at[spot], rs.at[i], rr.at[spot], (i, 2 * x + host), MESH),
            pltpu.make_async_copy(best.at[lax.div(i, 4)], large_in.at[spot], rr.at[spot]),
        )

    @pl.when(busy)
    def _():
        share(7)
        compare(6)
        compare(7)

        def give(i, carry):
            far, near = result_copies(i)

            @pl.when(jnp.logical_not((i == b) & (host == core)))
            def _():
                far.start()

            @pl.when((i == b) & (host == core))
            def _():
                near.start()

            return carry

        lax.fori_loop(0, 16, give, 0)

    lane_of = lax.div(iota((8, SLOT), 1), CAP)
    large = jnp.full((8, SLOT), -1.0, F32)
    for c in range(4):
        for h in range(2):
            pltpu.make_async_copy(large_in.at[2 * c + h], large_in.at[2 * c + h], rr.at[2 * c + h]).wait()
        shift = lax.rem(CAP * (c - y) + SLOT, SLOT)
        moved = pltpu.roll(jnp.maximum(large_in[2 * c], large_in[2 * c + 1]), shift, 1)
        large = jnp.where(lane_of == c, moved, large)
    for k in range(8):
        row = jnp.where(meta_recv[k, 0:1, :] < LARGE_IDS, large[k:k + 1], small_best[k:k + 1, :])
        final_send[k] = row

    def final_copy(k):
        return pltpu.make_async_remote_copy(
            final_send.at[k], final_recv.at[k], os.at[k], orr.at[k], (b, partner(k)), MESH)

    def final_start(k, carry):
        final_copy(k).start()
        return carry

    lax.fori_loop(1, 8, final_start, 0)
    final_recv[0] = final_send[0]

    def unpermute(k):
        out_ref[pl.ds(partner(k), 1), :] = jnp.sum(
            perms[k] * to_column(final_recv[k]), axis=0, keepdims=True)

    unpermute(0)

    def final_step(k, carry):
        final_copy(k).wait_recv()
        unpermute(k)
        return carry

    lax.fori_loop(1, 8, final_step, 0)

    def drain_line(k, carry):
        for copy in x_copies(k):
            copy.wait_send()
        final_copy(k).wait_send()
        return carry

    lax.fori_loop(1, 8, drain_line, 0)

    def drain_plane(k, carry):
        def piece(c, inner):
            far_rows, far_meta, _, _ = plane_copies(k, c)

            @pl.when(jnp.logical_not(is_self(c)))
            def _():
                far_rows.wait_send()
                far_meta.wait_send()

            return inner

        return lax.fori_loop(0, 4, piece, carry)

    lax.fori_loop(0, 8, drain_plane, 0)

    @pl.when(busy)
    def _():
        def drain_share(k, carry):
            for copy in share_copies(k):
                copy.wait_send()
            return carry

        lax.fori_loop(0, 8, drain_share, 0)

        def drain_result(i, carry):
            @pl.when(jnp.logical_not((i == b) & (host == core)))
            def _():
                result_copies(i)[0].wait_send()

            return carry

        lax.fori_loop(0, 16, drain_result, 0)


def shards(embeddings, cluster_ids, orders):
    dma = pltpu.SemaphoreType.DMA
    vmem = pltpu.VMEM
    out = pl.pallas_call(
        kernel,
        out_shape=jax.ShapeDtypeStruct((8, SLOT), F32),
        in_specs=[
            pl.BlockSpec(memory_space=pl.ANY),
            pl.BlockSpec(memory_space=pltpu.VMEM),
            pl.BlockSpec(memory_space=pltpu.VMEM),
        ],
        out_specs=pl.BlockSpec(memory_space=pltpu.VMEM),
        scratch_shapes=[
            vmem((8, SLOT, D), BF16),
            vmem((8, SLOT, D), BF16),
            vmem((8, SLOT, D), BF16),
            vmem((8, 8, SLOT), F32),
            vmem((8, 8, SLOT), F32),
            vmem((8, SLOT, SLOT), F32),
            vmem((8, 1, SLOT), F32),
            vmem((8, 512, D), BF16),
            vmem((8, 16, 1, SLOT), F32),
            vmem((8, 8, SLOT), F32),
            vmem((4, 8, SLOT), F32),
            vmem((8, 8, SLOT), F32),
            vmem((8, SLOT), F32),
            vmem((8, 1, SLOT), F32),
            vmem((8, 1, SLOT), F32),
            dma((8,)),
            dma((8,)), dma((8,)), dma((8,)), dma((8,)),
            dma((8, 4)), dma((8,)), dma((8, 4)), dma((8,)),
            dma((8,)), dma((8,)), dma((8,)), dma((8,)),
            dma((16,)), dma((8,)),
            dma((8,)), dma((8,)),
        ],
        compiler_params=pltpu.CompilerParams(
            collective_id=0, has_side_effects=True, vmem_limit_bytes=40 * 1024 * 1024),
    )(embeddings.reshape(8, SLOT, D), cluster_ids.reshape(8, SLOT), orders.reshape(8, SLOT))
    return out.reshape(1, 1, 8, SLOT)


def solution(mesh):
    in_specs = (
        P("blk", "group", None, None, None),
        P("blk", "group", None, None),
        P("blk", "group", None, None),
    )
    out_specs = P("blk", "group", None, None)
    return jax.shard_map(shards, mesh=mesh, in_specs=in_specs, out_specs=out_specs, check_vma=False)
```

time: 271 us -> 83.9 us (0.31)
  waiting for transfers between devices: 108 us -> 0 us
  Pallas kernels: 0 us -> 80.4 us
  blocking collectives: 75.8 us -> 0 us
  matrix products: 61.2 us -> 0 us
  between operations: 13.4 us -> 0.01 us
  starting transfers between devices: 8.18 us -> 0 us
    all_gather x1 -> x0, waiting for transfers between devices: 103 us -> none  [shards(): keys = lax.all_gather(unit, 'blk', axis=0, tiled=True)]
    pallas_call x0 -> x1, Pallas kernels: none -> 80.4 us  [shards(): pl.pallas_call(kernel, out_shape=jax.ShapeDtypeStruct((8, SLOT), F32), in...]
    dot_general x16 -> x0, matrix products: 61.2 us -> none  [block_scores(): lax.dot_general(query, keys, (((1,), (1,)), ((), ())), preferred_element_...]
    all_gather x2 -> x0, blocking collectives: 39.9 us -> none  [the longest x1 21.9 us: shards(): key_ids = lax.all_gather(ident, 'blk', axis=0, tiled=True)]
    all_to_all x2 -> x0, blocking collectives: 35.9 us -> none  [the longest x1 26.6 us: shards(): lax.all_to_all(embeddings, 'group', split_axis=2, concat_axis=1, tiled=True)]
    all_to_all x2 -> x0, starting transfers between devices: 8.18 us -> none  [the longest x1 4.26 us: shards(): lax.all_to_all(cluster_ids, 'group', split_axis=2, concat_axis=1, tiled=T...]
    all_to_all x2 -> x0, waiting for transfers between devices: 4.52 us -> none  [the longest x1 4.52 us: shards(): lax.all_to_all(cluster_ids, 'group', split_axis=2, concat_axis=1, tiled=T...]
    unnamed x1 -> x7, local copies, waits for them, and re-layouts: 0.59 us -> 3.38 us
  transfers between devices with their start and end apart: 3 -> 0, of which waited for: 2 -> 0; matrix products, arithmetic and copies ran while one was open for 0% -> 0% of each run, Pallas kernels for 0% -> 0%
where the time goes in v1:
time: 83.9 us; the launch traced here: 83.8 us
  Pallas kernels  80.4 us (96%)
  local copies, waits for them, and re-layouts  3.38 us (4%)
    pallas_call x1, Pallas kernels, shards(): pl.pallas_call(kernel, out_shape=jax.ShapeDtypeStruct((8, SLOT), F32), in...  80.4 us
    unnamed x7, local copies, waits for them, and re-layouts  3.38 us

profile of v1, /device:TPU:1, one launch (start us, length us, event | category | flops | bytes accessed | tf_op | source)
XLA Modules:
  0.0 83.8 jit_solution(8567515814644846884)
XLA Ops:
  0.0 0.0 copy-start
  0.0 1.4 %copy-done = bf16[1,1,8,128,768]{4,3,2,1,0:T(8,128)(2,1)S(1)} copy-done((bf16[1,1,8,128,768]{4,3,2,1,0:T(8,128)(2,1)S(1)}, bf16[1,1,8,128,768]{4,3,2,1,0:T(8,128)(2,1)}, u32[]{:S(2)}) %copy-start) | copy-done | bytes 1572888
  1.4 0.0 copy-start.1
  1.4 0.7 copy-done.1
  2.1 0.0 copy-start.2
  2.1 0.7 copy-done.2
  2.8 80.4 %shard_map.37 = f32[8,128]{1,0:T(8,128)S(1)} custom-call(bf16[8,128,768]{2,1,0:T(8,128)(2,1)S(1)} %bitcast.4, s32[8,128]{1,0:T(8,128)S(1)} %bitcast.6, s32[8,128]{1,0:T(8,128)S(1)} %bitcast.7), custom_call_target="tpu_custom_call" | custom-call | tf_op jit(solution)/shard_map/pallas_call | solution.py:420
  83.2 0.6 copy.5
Async XLA Ops:
  0.0 1.4 %copy-start = (bf16[1,1,8,128,768]{4,3,2,1,0:T(8,128)(2,1)S(1)}, bf16[1,1,8,128,768]{4,3,2,1,0:T(8,128)(2,1)}, u32[]{:S(2)}) copy-start(bf16[1,1,8,128,768]{4,3,2,1,0:T(8,128)(2,1)} %param.3) | copy-start | bytes 4718596
  1.4 0.7 copy-start.1
  2.1 0.7 copy-start.2

commit v2 on v1

v2 whole, which is shorter than its diff:
```python
import jax
import jax.numpy as jnp
from jax import lax
from jax.experimental import pallas as pl
from jax.experimental.pallas import tpu as pltpu
from jax.sharding import PartitionSpec as P

MESH = pl.DeviceIdType.MESH
F32 = jnp.float32
BF16 = jnp.bfloat16
D = 768
SLOT = 128
CAP = 32
LARGE_IDS = 32.0
NEVER = 1.0e9
EARLY = 5
LAG = 3


def flip(value, bits):
    out = 0
    for shift in (1, 2, 4):
        bit = lax.rem(lax.div(value, shift), 2) + lax.rem(lax.div(bits, shift), 2)
        out = out + shift * lax.rem(bit, 2)
    return out


def iota(shape, dim):
    return lax.broadcasted_iota(jnp.int32, shape, dim)


def to_column(row):
    eye = iota((SLOT, SLOT), 0) == iota((SLOT, SLOT), 1)
    return jnp.sum(jnp.where(eye, jnp.broadcast_to(row, (SLOT, SLOT)), 0.0), axis=1, keepdims=True)


def to_row(column):
    eye = iota((SLOT, SLOT), 0) == iota((SLOT, SLOT), 1)
    return jnp.sum(jnp.where(eye, jnp.broadcast_to(column, (SLOT, SLOT)), 0.0), axis=0, keepdims=True)


def product(query, keys):
    return lax.dot_general(query, keys, (((1,), (1,)), ((), ())), preferred_element_type=F32)


def permutation(ids, group):
    large = ids < LARGE_IDS
    label = jnp.where(large, ids - 4.0 * group.astype(F32), 4.0)
    sub = iota((SLOT, SLOT), 0)
    lane = iota((SLOT, SLOT), 1)
    before = jnp.where((to_column(label) == label) & (sub < lane), 1.0, 0.0)
    rank = jnp.sum(before, axis=0, keepdims=True)
    dest = jnp.where(large, CAP * label + rank, 4096.0)
    subf = sub.astype(F32)
    taken = jnp.where(dest == subf, 1024.0, 0.0) + jnp.where(dest < subf, 1.0, 0.0)
    slot = iota((SLOT, 1), 0).astype(F32)
    free = slot - jnp.sum(taken, axis=1, keepdims=True)
    return jnp.where((dest == subf) | (free == jnp.where(large, -8192.0, rank)), 1.0, 0.0)


def permuted_meta(ids, orders, perm):
    id_high = jnp.floor(ids * (1.0 / 32))
    order_high = jnp.floor(orders * (1.0 / 1024))
    rest = orders - 1024.0 * order_high
    order_mid = jnp.floor(rest * (1.0 / 32))
    at = iota((8, SLOT), 0)
    parts = jnp.zeros((8, SLOT), F32)
    pieces = (id_high, ids - 32.0 * id_high, order_high, order_mid, rest - 32.0 * order_mid)
    for index, piece in enumerate(pieces):
        parts = jnp.where(at == index, jnp.broadcast_to(piece, (8, SLOT)), parts)
    moved = product(parts, perm)
    slot_ids = moved[0:1] * 32.0 + moved[1:2]
    slot_orders = moved[2:3] * 1024.0 + moved[3:4] * 32.0 + moved[4:5]
    large_orders = jnp.where(slot_ids < LARGE_IDS, slot_orders, NEVER)
    out = jnp.where(at == 0, jnp.broadcast_to(slot_ids, (8, SLOT)), jnp.broadcast_to(slot_orders, (8, SLOT)))
    return jnp.where(at == 2, jnp.broadcast_to(large_orders, (8, SLOT)), out)


def kernel(
    emb, ids_in, orders_in, out_ref,
    raw, ids_ref, orders_ref, send, recv, meta_send, meta_recv, perms, plane_meta, mid, mid_meta,
    keys, key_meta, key_orders, best, found_ref, tile_send, large_in, small_best, final_send, final_recv,
    load_sem, info_sem, xs, xr, xms, xmr, ps, pr, pms, pmr, ss, sr, sms, smr, fs, fr, fms, fmr,
    ts, tr, os, orr,
):
    b = lax.axis_index("blk")
    g = lax.axis_index("group")
    z, y = lax.div(b, 4), lax.rem(b, 4)
    x, core = lax.div(g, 2), lax.rem(g, 2)
    offset = lax.rem(y - z + 4, 4)
    busy = lax.rem(offset, 2) == 0
    host = lax.div(offset, 2)

    def relation(k):
        return lax.rem(3 * k, 8)

    def partner(k):
        return flip(g, relation(k))

    def load(k):
        return pltpu.make_async_copy(emb.at[partner(k)], raw.at[k], load_sem.at[k])

    info = (
        pltpu.make_async_copy(ids_in, ids_ref, info_sem.at[0]),
        pltpu.make_async_copy(orders_in, orders_ref, info_sem.at[1]),
    )
    for copy in info:
        copy.start()

    def load_step(k, carry):
        load(k).start()
        return carry

    lax.fori_loop(0, 8, load_step, 0)

    barrier = pltpu.get_barrier_semaphore()

    def greet(blk, group):
        pl.semaphore_signal(barrier, inc=1, device_id=(blk, group), device_id_type=MESH)

    for step in range(1, 4):
        for h in range(2):
            greet(4 * lax.rem(z + step, 4) + y, 2 * x + h)
            greet(4 * z + lax.rem(y + step, 4), 2 * x + h)
            greet(b, 2 * lax.rem(x + step, 4) + h)
    greet(b, 2 * x + 1 - core)

    def prepare(k):
        load(k).wait()
        owner = partner(k)
        ids = ids_ref[pl.ds(owner, 1), :].astype(F32)
        orders = orders_ref[pl.ds(owner, 1), :].astype(F32)
        perm = permutation(ids, owner)
        perms[k] = perm
        values = raw[k].astype(F32)
        total = jnp.sum(values * values, axis=1, keepdims=True)
        unit = (values * lax.rsqrt(total + 1e-06)).astype(BF16)
        rows = jnp.dot(perm.astype(BF16), unit, preferred_element_type=F32).astype(BF16)
        return rows, permuted_meta(ids, orders, perm)

    def block_of(k):
        return pl.ds(pl.multiple_of(k * SLOT, SLOT), SLOT)

    def x_copies(k):
        to = (b, partner(k))
        return (
            pltpu.make_async_remote_copy(send.at[k], recv.at[block_of(k)], xs.at[k], xr.at[k], to, MESH),
            pltpu.make_async_remote_copy(meta_send.at[k], meta_recv.at[k], xms.at[k], xmr.at[k], to, MESH),
        )

    def axes(k):
        odd = lax.rem(k, 2) == 1
        return odd, jnp.where(odd, z, y), jnp.where(odd, y, z)

    def device_at(odd, a, bb):
        return jnp.where(odd, 4 * a + bb, 4 * bb + a)

    def first_way(k, t):
        odd, a, bb = axes(k)
        end = lax.rem(t + 2 * core, 4)
        turned = (lax.rem(bb - end + 4, 4) == 2) & (lax.rem(a - t + 4, 2) == 1)
        return turned, device_at(odd, jnp.where(turned, a, t), jnp.where(turned, end, bb))

    def first_copies(k, t):
        odd, a, _ = axes(k)
        turned, stop = first_way(k, t)
        c = jnp.where(odd, t, lax.rem(t + 2 * core, 4))
        at = jnp.where(turned, 4, a)
        which = jnp.where(turned, 1, 0)
        rows = pl.ds(pl.multiple_of(k * SLOT + c * CAP, CAP), CAP)
        spot = pl.ds(pl.multiple_of(at * CAP, CAP), CAP)
        return (
            pltpu.make_async_remote_copy(
                recv.at[rows], mid.at[k, spot], ps.at[k, t], pr.at[k, which], (stop, g), MESH),
            pltpu.make_async_remote_copy(
                plane_meta.at[k], mid_meta.at[k, at], pms.at[k, t], pmr.at[k, which], (stop, g), MESH),
        )

    def first_near(k):
        odd, a, _ = axes(k)
        c = jnp.where(odd, a, lax.rem(a + 2 * core, 4))
        rows = pl.ds(pl.multiple_of(k * SLOT + c * CAP, CAP), CAP)
        spot = pl.ds(pl.multiple_of(a * CAP, CAP), CAP)
        return (
            pltpu.make_async_copy(recv.at[rows], mid.at[k, spot], pr.at[k, 0]),
            pltpu.make_async_copy(plane_meta.at[k], mid_meta.at[k, a], pmr.at[k, 0]),
        )

    def send_first(k):
        plane_meta[k] = meta_recv[k, 2:3, :]
        _, a, _ = axes(k)

        def piece(step, carry):
            rows, meta = first_copies(k, lax.rem(a + step, 4))
            meta.start()
            rows.start()
            return carry

        lax.fori_loop(1, 4, piece, 0)
        for copy in first_near(k):
            copy.start()

    def piece_copies(k, source, place, blk, sem):
        to = (blk, 2 * x + lax.div(place, 8))
        rows = pl.ds(pl.multiple_of(source * CAP, CAP), CAP)
        spot = pl.ds(pl.multiple_of(place * CAP, CAP), CAP)
        return (
            pltpu.make_async_remote_copy(
                mid.at[k, rows], keys.at[k, spot], ss.at[k, sem], sr.at[k], to, MESH),
            pltpu.make_async_remote_copy(
                mid_meta.at[k, source], key_meta.at[k, place], sms.at[k, sem], smr.at[k], to, MESH),
        )

    def block_copies(k):
        odd, a, bb = axes(k)
        blk = device_at(odd, a, lax.rem(a + 2 * core, 4))
        to = (blk, 2 * x + lax.div(bb, 2))
        rows = mid.at[k, pl.ds(0, SLOT)]
        spot = keys.at[k, pl.ds(pl.multiple_of(bb * SLOT, SLOT), SLOT)]
        meta = mid_meta.at[k, pl.ds(0, 4)]
        meta_spot = key_meta.at[k, pl.ds(pl.multiple_of(bb * 4, 4), 4)]
        return (
            pltpu.make_async_remote_copy(rows, spot, ss.at[k, 0], sr.at[k], to, MESH),
            pltpu.make_async_remote_copy(meta, meta_spot, sms.at[k, 0], smr.at[k], to, MESH),
            pltpu.make_async_copy(rows, spot, sr.at[k]),
            pltpu.make_async_copy(meta, meta_spot, smr.at[k]),
        )

    def second_kind(k):
        _, a, bb = axes(k)
        split = lax.rem(bb - a - 2 * core + 8, 4) == 2
        stays = busy & (host == core) & (lax.div(bb, 2) == core)
        return split, stays

    def split_copies(k, n):
        odd, a, bb = axes(k)
        source = lax.rem(a + 2 * n, 4)
        return piece_copies(k, source, 4 * bb + source, device_at(odd, a, lax.rem(a + 2 * core, 4)), n)

    def turned_copies(k):
        odd, a, bb = axes(k)
        blk = device_at(odd, lax.rem(bb + 2 * core, 4), bb)
        return piece_copies(k, 4, 4 * lax.rem(bb + 2, 4) + a, blk, 1)

    def send_second(k):
        split, stays = second_kind(k)

        @pl.when(split)
        def _():
            half_meta = mid_meta.at[k, pl.ds(0, 2)]
            half_rows = mid.at[k, pl.ds(0, 2 * CAP)]
            pltpu.make_async_copy(half_meta, half_meta, pmr.at[k, 0]).wait()
            pltpu.make_async_copy(half_rows, half_rows, pr.at[k, 0]).wait()
            for n in range(2):
                rows, meta = split_copies(k, n)
                meta.start()
                rows.start()

        @pl.when(jnp.logical_not(split))
        def _():
            all_meta = mid_meta.at[k, pl.ds(0, 4)]
            all_rows = mid.at[k, pl.ds(0, SLOT)]
            pltpu.make_async_copy(all_meta, all_meta, pmr.at[k, 0]).wait()
            pltpu.make_async_copy(all_rows, all_rows, pr.at[k, 0]).wait()
            far_rows, far_meta, near_rows, near_meta = block_copies(k)

            @pl.when(jnp.logical_not(stays))
            def _():
                far_meta.start()
                far_rows.start()

            @pl.when(stays)
            def _():
                near_meta.start()
                near_rows.start()

        @pl.when(jnp.logical_not(busy))
        def _():
            rows, meta = turned_copies(k)
            one_meta = mid_meta.at[k, 4]
            one_rows = mid.at[k, pl.ds(4 * CAP, CAP)]
            pltpu.make_async_copy(one_meta, one_meta, pmr.at[k, 1]).wait()
            pltpu.make_async_copy(one_rows, one_rows, pr.at[k, 1]).wait()
            meta.start()
            rows.start()

    def share_copies(k):
        to = (b, 2 * x + 1 - core)
        rows = pl.ds(pl.multiple_of(core * 256, 256), 256)
        sources = pl.ds(pl.multiple_of(core * 8, 8), 8)
        return (
            pltpu.make_async_remote_copy(keys.at[k, rows], keys.at[k, rows], fs.at[k], fr.at[k], to, MESH),
            pltpu.make_async_remote_copy(
                key_meta.at[k, sources], key_meta.at[k, sources], fms.at[k], fmr.at[k], to, MESH),
        )

    def share(k):
        rows = keys.at[k, pl.ds(pl.multiple_of(core * 256, 256), 256)]
        sources = key_meta.at[k, pl.ds(pl.multiple_of(core * 8, 8), 8)]
        pltpu.make_async_copy(sources, sources, smr.at[k]).wait()
        pltpu.make_async_copy(rows, rows, sr.at[k]).wait()
        for copy in share_copies(k):
            copy.start()

    lane_part = lax.div(iota((1, SLOT), 1), CAP)

    def merge_orders(k, u):
        merged = jnp.zeros((1, SLOT), F32)
        for j in range(4):
            shift = lax.rem(CAP * (j - z) + SLOT, SLOT)
            merged = jnp.where(lane_part == j, pltpu.roll(key_meta[k, 4 * u + j], shift, 1), merged)
        key_orders[k, pl.ds(u, 1), :] = merged

    def query_of(k):
        places = [to_column(key_orders[k, pl.ds(2 * core + i, 1), :]) for i in range(2)]
        return keys[k, pl.ds(pl.multiple_of(core * 256, 256), 256)], jnp.concatenate(places, axis=0)

    def against(query, places, j, found, one_way):
        for h in range(2):
            scores = product(query, keys[j, h * 256:(h + 1) * 256])
            for i in range(2):
                u = 2 * h + i
                part = scores[:, i * SLOT:(i + 1) * SLOT]
                earlier = key_orders[j, u:u + 1, :] < places
                found = jnp.maximum(found, jnp.where(earlier, part, -1.0))
                if not one_way:
                    other = jnp.max(jnp.where(earlier, -1.0, part), axis=0, keepdims=True)
                    best[u, pl.ds(j, 1), :] = jnp.maximum(best[u, pl.ds(j, 1), :], other)
        return found

    def compare_old(k):
        for i in range(2):
            merge_orders(k, 2 * core + i)
        query, places = query_of(k)
        start = jnp.full((256, SLOT), -1.0, F32)
        if isinstance(k, int):
            found = start
            for j in range(k):
                found = against(query, places, j, found, False)
            found_ref[...] = found
            return

        def two(j, found):
            return against(query, places, 2 * j + 1, against(query, places, 2 * j, found, False), False)

        found_ref[...] = lax.fori_loop(0, lax.div(k, 2), two, start)

        @pl.when(lax.rem(k, 2) == 1)
        def _():
            found_ref[...] = against(query, places, k - 1, found_ref[...], False)

    def compare_same(k):
        for copy in share_copies(k):
            copy.wait_recv()
        for i in range(2):
            merge_orders(k, 2 * (1 - core) + i)
        query, places = query_of(k)
        found = against(query, places, k, found_ref[...], True)
        column = jnp.max(found, axis=1, keepdims=True)
        for i in range(2):
            best[2 * core + i, pl.ds(k, 1), :] = to_row(column[i * SLOT:(i + 1) * SLOT])

    def take(k):
        share(k)
        if not isinstance(k, int):
            pl.when(k >= 1)(lambda: compare_same(k - 1))
        elif k >= 1:
            compare_same(k - 1)
        compare_old(k)

    best[...] = jnp.full(best.shape, -1.0, F32)
    for copy in info:
        copy.wait()

    rows, meta = prepare(0)
    recv[0:SLOT] = rows
    meta_recv[0] = meta

    def prepare_step(k, carry):
        rows, meta = prepare(k)
        send[k] = rows
        meta_send[k] = meta
        return carry

    def leave_step(k, carry):
        for copy in x_copies(k):
            copy.start()
        return carry

    lax.fori_loop(1, EARLY, prepare_step, 0)
    pl.semaphore_wait(barrier, 19)
    lax.fori_loop(1, EARLY, leave_step, 0)
    send_first(0)
    lax.fori_loop(EARLY, 8, lambda k, carry: leave_step(k, prepare_step(k, carry)), 0)

    def pass_on(k, carry):
        for copy in x_copies(k):
            copy.wait_recv()
        send_first(k)
        send_second(k - 1)

        @pl.when(busy & (k >= LAG))
        def _():
            take(k - LAG)

        return carry

    lax.fori_loop(1, 8, pass_on, 0)
    send_second(7)

    def small(q, carry):
        query = recv[pl.ds(pl.multiple_of(q * 256, 256), 256)]
        labels = jnp.concatenate([to_column(meta_recv[2 * q + i, 0:1, :]) for i in range(2)], axis=0)
        labels = jnp.where(labels < LARGE_IDS, -1.0, labels)
        places = jnp.concatenate([to_column(meta_recv[2 * q + i, 1:2, :]) for i in range(2)], axis=0)
        found = jnp.full((256, SLOT), -1.0, F32)
        for j in range(4):
            scores = product(query, recv[j * 256:(j + 1) * 256])
            for i in range(2):
                match = (meta_recv[2 * j + i, 0:1, :] == labels) & (meta_recv[2 * j + i, 1:2, :] < places)
                found = jnp.maximum(found, jnp.where(match, scores[:, i * SLOT:(i + 1) * SLOT], -1.0))
        column = jnp.max(found, axis=1, keepdims=True)
        for i in range(2):
            small_best[pl.ds(2 * q + i, 1), :] = to_row(column[i * SLOT:(i + 1) * SLOT])
        return carry

    lax.fori_loop(0, 4, small, 0)

    def result_copies(i):
        spot = 2 * z + core
        return (
            pltpu.make_async_remote_copy(
                tile_send.at[i], large_in.at[spot], ts.at[i], tr.at[spot], (i, 2 * x + host), MESH),
            pltpu.make_async_copy(tile_send.at[i], large_in.at[spot], tr.at[spot]),
        )

    even = lax.rem(iota((8, SLOT), 0), 2) == 0

    @pl.when(busy)
    def _():
        if LAG > 2:
            lax.fori_loop(8 - LAG, 6, lambda k, carry: (take(k), carry)[1], 0)
        take(6)
        take(7)
        compare_same(7)
        for i in range(16):
            tile_send[i] = jnp.where(even, best[i // 4], best[i % 4])
            far, near = result_copies(i)
            mine = (b == i) & (host == core)
            pl.when(jnp.logical_not(mine))(far.start)
            pl.when(mine)(near.start)

    lane_of = lax.div(iota((8, SLOT), 1), CAP)
    large = jnp.full((8, SLOT), -1.0, F32)
    for c in range(4):
        for h in range(2):
            pltpu.make_async_copy(large_in.at[2 * c + h], large_in.at[2 * c + h], tr.at[2 * c + h]).wait()
        joined = jnp.maximum(large_in[2 * c], large_in[2 * c + 1])
        from_even = pltpu.roll(joined, lax.rem(CAP * (c - y) + SLOT, SLOT), 1)
        from_odd = pltpu.roll(joined, lax.rem(CAP * (c - z) + SLOT, SLOT), 1)
        large = jnp.where(lane_of == c, jnp.where(even, from_even, from_odd), large)
    for k in range(8):
        row = jnp.where(meta_recv[k, 0:1, :] < LARGE_IDS, large[k:k + 1], small_best[k:k + 1, :])
        final_send[k] = row

    def final_copy(k):
        return pltpu.make_async_remote_copy(
            final_send.at[k], final_recv.at[k], os.at[k], orr.at[k], (b, partner(k)), MESH)

    def final_start(k, carry):
        final_copy(k).start()
        return carry

    lax.fori_loop(1, 8, final_start, 0)
    final_recv[0] = final_send[0]

    def unpermute(k):
        out_ref[pl.ds(partner(k), 1), :] = jnp.sum(
            perms[k] * to_column(final_recv[k]), axis=0, keepdims=True)

    unpermute(0)

    def final_step(k, carry):
        final_copy(k).wait_recv()
        unpermute(k)
        return carry

    lax.fori_loop(1, 8, final_step, 0)

    def drain_line(k, carry):
        for copy in x_copies(k):
            copy.wait_send()
        final_copy(k).wait_send()
        return carry

    lax.fori_loop(1, 8, drain_line, 0)

    def drain_plane(k, carry):
        _, a, _ = axes(k)

        def piece(step, inner):
            for copy in first_copies(k, lax.rem(a + step, 4)):
                copy.wait_send()
            return inner

        lax.fori_loop(1, 4, piece, 0)
        split, stays = second_kind(k)

        @pl.when(split)
        def _():
            for n in range(2):
                for copy in split_copies(k, n):
                    copy.wait_send()

        @pl.when(jnp.logical_not(split | stays))
        def _():
            for copy in block_copies(k)[:2]:
                copy.wait_send()

        @pl.when(jnp.logical_not(busy))
        def _():
            for copy in turned_copies(k):
                copy.wait_send()

        return carry

    lax.fori_loop(0, 8, drain_plane, 0)

    @pl.when(busy)
    def _():
        def drain_share(k, carry):
            for copy in share_copies(k):
                copy.wait_send()
            return carry

        lax.fori_loop(0, 8, drain_share, 0)
        for i in range(16):
            pl.when(jnp.logical_not((b == i) & (host == core)))(result_copies(i)[0].wait_send)


def shards(embeddings, cluster_ids, orders):
    dma = pltpu.SemaphoreType.DMA
    vmem = pltpu.VMEM
    out = pl.pallas_call(
        kernel,
        out_shape=jax.ShapeDtypeStruct((8, SLOT), F32),
        in_specs=[pl.BlockSpec(memory_space=pl.ANY)] * 3,
        out_specs=pl.BlockSpec(memory_space=pltpu.VMEM),
        scratch_shapes=[
            vmem((8, SLOT, D), BF16),
            vmem((8, SLOT), jnp.int32),
            vmem((8, SLOT), jnp.int32),
            vmem((8, SLOT, D), BF16),
            vmem((8 * SLOT, D), BF16),
            vmem((8, 8, SLOT), F32),
            vmem((8, 8, SLOT), F32),
            vmem((8, SLOT, SLOT), F32),
            vmem((8, 1, SLOT), F32),
            vmem((8, 5 * CAP, D), BF16),
            vmem((8, 5, 1, SLOT), F32),
            vmem((8, 512, D), BF16),
            vmem((8, 16, 1, SLOT), F32),
            vmem((8, 8, SLOT), F32),
            vmem((4, 8, SLOT), F32),
            vmem((256, SLOT), F32),
            vmem((16, 8, SLOT), F32),
            vmem((8, 8, SLOT), F32),
            vmem((8, SLOT), F32),
            vmem((8, 1, SLOT), F32),
            vmem((8, 1, SLOT), F32),
            dma((8,)), dma((2,)),
            dma((8,)), dma((8,)), dma((8,)), dma((8,)),
            dma((8, 4)), dma((8, 2)), dma((8, 4)), dma((8, 2)),
            dma((8, 2)), dma((8,)), dma((8, 2)), dma((8,)),
            dma((8,)), dma((8,)), dma((8,)), dma((8,)),
            dma((16,)), dma((8,)),
            dma((8,)), dma((8,)),
        ],
        compiler_params=pltpu.CompilerParams(
            collective_id=0, has_side_effects=True, vmem_limit_bytes=60 * 1024 * 1024),
    )(embeddings.reshape(8, SLOT, D), cluster_ids.reshape(8, SLOT), orders.reshape(8, SLOT))
    return out.reshape(1, 1, 8, SLOT)


def solution(mesh):
    in_specs = (
        P("blk", "group", None, None, None),
        P("blk", "group", None, None),
        P("blk", "group", None, None),
    )
    out_specs = P("blk", "group", None, None)
    return jax.shard_map(shards, mesh=mesh, in_specs=in_specs, out_specs=out_specs, check_vma=False)
```

time: 83.9 us -> 61.8 us (0.74)
  Pallas kernels: 80.4 us -> 60.3 us
  local copies, waits for them, and re-layouts: 3.38 us -> 1.28 us
    pallas_call x1, Pallas kernels: 80.4 us -> 60.3 us  [shards(): pl.pallas_call(kernel, out_shape=jax.ShapeDtypeStruct((8, SLOT), F32), in...]
    unnamed x7 -> x1, local copies, waits for them, and re-layouts: 3.38 us -> 1.28 us
where the time goes in v2:
time: 61.8 us; the launch traced here: 61.6 us
  Pallas kernels  60.3 us (98%)
  local copies, waits for them, and re-layouts  1.28 us (2%)
    pallas_call x1, Pallas kernels, shards(): pl.pallas_call(kernel, out_shape=jax.ShapeDtypeStruct((8, SLOT), F32), in...  60.3 us
    unnamed x1, local copies, waits for them, and re-layouts  1.28 us

profile of v2, /device:TPU:1, one launch (start us, length us, event | category | flops | bytes accessed | tf_op | source)
XLA Modules:
  0.0 61.6 jit_solution(2205412465723141379)
XLA Ops:
  0.0 60.3 %shard_map.37 = f32[8,128]{1,0:T(8,128)} custom-call(bf16[8,128,768]{2,1,0:T(8,128)(2,1)} %bitcast.4, s32[8,128]{1,0:T(8,128)} %bitcast.6, s32[8,128]{1,0:T(8,128)} %bitcast.7), custom_call_target="tpu_custom_call" | custom-call | tf_op jit(solution)/shard_map/pallas_call | solution.py:544
  60.3 1.3 %copy.5 = f32[1,1,8,128]{3,2,1,0:T(8,128)} copy(f32[1,1,8,128]{3,2,1,0:T(8,128)} %bitcast.5) | data formatting | bytes 8192

commit v3 on v2

--- a/solution.py
+++ b/solution.py
@@ -14,7 +14,9 @@
 LARGE_IDS = 32.0
 NEVER = 1.0e9
 EARLY = 5
-LAG = 3
+LAG = 4
+PASS = 2
+ORDER = sum(way << (3 * step) for step, way in enumerate((0, 1, 2, 6, 3, 7, 4, 5)))
 
 
 def flip(value, bits):
@@ -81,7 +83,7 @@
     raw, ids_ref, orders_ref, send, recv, meta_send, meta_recv, perms, plane_meta, mid, mid_meta,
     keys, key_meta, key_orders, best, found_ref, tile_send, large_in, small_best, final_send, final_recv,
     load_sem, info_sem, xs, xr, xms, xmr, ps, pr, pms, pmr, ss, sr, sms, smr, fs, fr, fms, fmr,
-    ts, tr, os, orr,
+    ts, tr, os, orr, ready,
 ):
     b = lax.axis_index("blk")
     g = lax.axis_index("group")
@@ -92,7 +94,7 @@
     host = lax.div(offset, 2)
 
     def relation(k):
-        return lax.rem(3 * k, 8)
+        return lax.rem(lax.div(ORDER, lax.shift_left(1, 3 * k)), 8)
 
     def partner(k):
         return flip(g, relation(k))
@@ -149,22 +151,22 @@
         )
 
     def axes(k):
-        odd = lax.rem(k, 2) == 1
-        return odd, jnp.where(odd, z, y), jnp.where(odd, y, z)
-
-    def device_at(odd, a, bb):
-        return jnp.where(odd, 4 * a + bb, 4 * bb + a)
+        staged = lax.rem(k, 2) == 0
+        return staged, jnp.where(staged, z, y), jnp.where(staged, y, z)
+
+    def device_at(staged, a, bb):
+        return jnp.where(staged, 4 * a + bb, 4 * bb + a)
 
     def first_way(k, t):
-        odd, a, bb = axes(k)
+        staged, a, bb = axes(k)
         end = lax.rem(t + 2 * core, 4)
         turned = (lax.rem(bb - end + 4, 4) == 2) & (lax.rem(a - t + 4, 2) == 1)
-        return turned, device_at(odd, jnp.where(turned, a, t), jnp.where(turned, end, bb))
+        return turned, device_at(staged, jnp.where(turned, a, t), jnp.where(turned, end, bb))
 
     def first_copies(k, t):
-        odd, a, _ = axes(k)
+        staged, a, _ = axes(k)
         turned, stop = first_way(k, t)
-        c = jnp.where(odd, t, lax.rem(t + 2 * core, 4))
+        c = jnp.where(staged, t, lax.rem(t + 2 * core, 4))
         at = jnp.where(turned, 4, a)
         which = jnp.where(turned, 1, 0)
         rows = pl.ds(pl.multiple_of(k * SLOT + c * CAP, CAP), CAP)
@@ -177,8 +179,8 @@
         )
 
     def first_near(k):
-        odd, a, _ = axes(k)
-        c = jnp.where(odd, a, lax.rem(a + 2 * core, 4))
+        staged, a, _ = axes(k)
+        c = jnp.where(staged, a, lax.rem(a + 2 * core, 4))
         rows = pl.ds(pl.multiple_of(k * SLOT + c * CAP, CAP), CAP)
         spot = pl.ds(pl.multiple_of(a * CAP, CAP), CAP)
         return (
@@ -186,19 +188,64 @@
             pltpu.make_async_copy(plane_meta.at[k], mid_meta.at[k, a], pmr.at[k, 0]),
         )
 
+    def direct_copies(k, t):
+        c = lax.rem(t + 2 * core, 4)
+        to = (4 * c + t, 2 * x + lax.div(z, 2))
+        rows = recv.at[pl.ds(pl.multiple_of(k * SLOT + c * CAP, CAP), CAP)]
+        spot = keys.at[k, pl.ds(pl.multiple_of(b * CAP, CAP), CAP)]
+        meta, meta_spot = plane_meta.at[k], key_meta.at[k, b]
+        return (
+            pltpu.make_async_remote_copy(rows, spot, ps.at[k, t], sr.at[k], to, MESH),
+            pltpu.make_async_remote_copy(meta, meta_spot, pms.at[k, t], smr.at[k], to, MESH),
+            pltpu.make_async_copy(rows, spot, sr.at[k]),
+            pltpu.make_async_copy(meta, meta_spot, smr.at[k]),
+        )
+
+    def direct_near(t):
+        return (4 * lax.rem(t + 2 * core, 4) + t == b) & (lax.div(z, 2) == core)
+
     def send_first(k):
         plane_meta[k] = meta_recv[k, 2:3, :]
-        _, a, _ = axes(k)
+        staged, a, _ = axes(k)
 
         def piece(step, carry):
-            rows, meta = first_copies(k, lax.rem(a + step, 4))
-            meta.start()
-            rows.start()
+            t = lax.rem(a + step, 4)
+            turned, _ = first_way(k, t)
+
+            @pl.when(staged | turned)
+            def _():
+                rows, meta = first_copies(k, t)
+                meta.start()
+                rows.start()
+
+            @pl.when(jnp.logical_not(staged | turned | direct_near(t)))
+            def _():
+                rows, meta, _, _ = direct_copies(k, t)
+                meta.start()
+                rows.start()
+
             return carry
 
         lax.fori_loop(1, 4, piece, 0)
-        for copy in first_near(k):
-            copy.start()
+
+        @pl.when(staged)
+        def _():
+            for copy in first_near(k):
+                copy.start()
+
+        @pl.when(jnp.logical_not(staged))
+        def _():
+            far_rows, far_meta, near_rows, near_meta = direct_copies(k, a)
+
+            @pl.when(direct_near(a))
+            def _():
+                near_meta.start()
+                near_rows.start()
+
+            @pl.when(jnp.logical_not(direct_near(a)))
+            def _():
+                far_meta.start()
+                far_rows.start()
 
     def piece_copies(k, source, place, blk, sem):
         to = (blk, 2 * x + lax.div(place, 8))
@@ -212,8 +259,8 @@
         )
 
     def block_copies(k):
-        odd, a, bb = axes(k)
-        blk = device_at(odd, a, lax.rem(a + 2 * core, 4))
+        staged, a, bb = axes(k)
+        blk = device_at(staged, a, lax.rem(a + 2 * core, 4))
         to = (blk, 2 * x + lax.div(bb, 2))
         rows = mid.at[k, pl.ds(0, SLOT)]
         spot = keys.at[k, pl.ds(pl.multiple_of(bb * SLOT, SLOT), SLOT)]
@@ -233,19 +280,20 @@
         return split, stays
 
     def split_copies(k, n):
-        odd, a, bb = axes(k)
+        staged, a, bb = axes(k)
         source = lax.rem(a + 2 * n, 4)
-        return piece_copies(k, source, 4 * bb + source, device_at(odd, a, lax.rem(a + 2 * core, 4)), n)
+        return piece_copies(k, source, 4 * bb + source, device_at(staged, a, lax.rem(a + 2 * core, 4)), n)
 
     def turned_copies(k):
-        odd, a, bb = axes(k)
-        blk = device_at(odd, lax.rem(bb + 2 * core, 4), bb)
+        staged, a, bb = axes(k)
+        blk = device_at(staged, lax.rem(bb + 2 * core, 4), bb)
         return piece_copies(k, 4, 4 * lax.rem(bb + 2, 4) + a, blk, 1)
 
     def send_second(k):
+        staged, _, _ = axes(k)
         split, stays = second_kind(k)
 
-        @pl.when(split)
+        @pl.when(staged & split)
         def _():
             half_meta = mid_meta.at[k, pl.ds(0, 2)]
             half_rows = mid.at[k, pl.ds(0, 2 * CAP)]
@@ -256,7 +304,7 @@
                 meta.start()
                 rows.start()
 
-        @pl.when(jnp.logical_not(split))
+        @pl.when(staged & jnp.logical_not(split))
         def _():
             all_meta = mid_meta.at[k, pl.ds(0, 4)]
             all_rows = mid.at[k, pl.ds(0, SLOT)]
@@ -389,15 +437,18 @@
 
     lax.fori_loop(1, EARLY, prepare_step, 0)
     pl.semaphore_wait(barrier, 19)
+    for step in range(1, 4):
+        pl.semaphore_signal(ready, inc=1, device_id=(4 * lax.rem(z + step, 4) + y, g), device_id_type=MESH)
     lax.fori_loop(1, EARLY, leave_step, 0)
     send_first(0)
     lax.fori_loop(EARLY, 8, lambda k, carry: leave_step(k, prepare_step(k, carry)), 0)
+    pl.semaphore_wait(ready, 3)
 
     def pass_on(k, carry):
         for copy in x_copies(k):
             copy.wait_recv()
         send_first(k)
-        send_second(k - 1)
+        pl.when(k >= PASS)(lambda: send_second(k - PASS))
 
         @pl.when(busy & (k >= LAG))
         def _():
@@ -406,7 +457,7 @@
         return carry
 
     lax.fori_loop(1, 8, pass_on, 0)
-    send_second(7)
+    lax.fori_loop(8 - PASS, 8, lambda k, carry: (send_second(k), carry)[1], 0)
 
     def small(q, carry):
         query = recv[pl.ds(pl.multiple_of(q * 256, 256), 256)]
@@ -444,11 +495,67 @@
         take(7)
         compare_same(7)
         for i in range(16):
-            tile_send[i] = jnp.where(even, best[i // 4], best[i % 4])
+            tile_send[i] = jnp.where(even, best[i % 4], best[i // 4])
             far, near = result_copies(i)
             mine = (b == i) & (host == core)
             pl.when(jnp.logical_not(mine))(far.start)
             pl.when(mine)(near.start)
+
+    def drain_line(k, carry):
+        for copy in x_copies(k):
+            copy.wait_send()
+        return carry
+
+    lax.fori_loop(1, 8, drain_line, 0)
+
+    def drain_plane(k, carry):
+        staged, a, _ = axes(k)
+
+        def piece(step, inner):
+            t = lax.rem(a + step, 4)
+            for copy in first_copies(k, t):
+                copy.wait_send()
+            return inner
+
+        lax.fori_loop(1, 4, piece, 0)
+
+        @pl.when(jnp.logical_not(staged | direct_near(a)))
+        def _():
+            for copy in direct_copies(k, a)[:2]:
+                copy.wait_send()
+
+        split, stays = second_kind(k)
+
+        @pl.when(staged & split)
+        def _():
+            for n in range(2):
+                for copy in split_copies(k, n):
+                    copy.wait_send()
+
+        @pl.when(staged & jnp.logical_not(split | stays))
+        def _():
+            for copy in block_copies(k)[:2]:
+                copy.wait_send()
+
+        @pl.when(jnp.logical_not(busy))
+        def _():
+            for copy in turned_copies(k):
+                copy.wait_send()
+
+        return carry
+
+    lax.fori_loop(0, 8, drain_plane, 0)
+
+    @pl.when(busy)
+    def _():
+        def drain_share(k, carry):
+            for copy in share_copies(k):
+                copy.wait_send()
+            return carry
+
+        lax.fori_loop(0, 8, drain_share, 0)
+        for i in range(16):
+            pl.when(jnp.logical_not((b == i) & (host == core)))(result_copies(i)[0].wait_send)
 
     lane_of = lax.div(iota((8, SLOT), 1), CAP)
     large = jnp.full((8, SLOT), -1.0, F32)
@@ -456,8 +563,8 @@
         for h in range(2):
             pltpu.make_async_copy(large_in.at[2 * c + h], large_in.at[2 * c + h], tr.at[2 * c + h]).wait()
         joined = jnp.maximum(large_in[2 * c], large_in[2 * c + 1])
-        from_even = pltpu.roll(joined, lax.rem(CAP * (c - y) + SLOT, SLOT), 1)
-        from_odd = pltpu.roll(joined, lax.rem(CAP * (c - z) + SLOT, SLOT), 1)
+        from_even = pltpu.roll(joined, lax.rem(CAP * (c - z) + SLOT, SLOT), 1)
+        from_odd = pltpu.roll(joined, lax.rem(CAP * (c - y) + SLOT, SLOT), 1)
         large = jnp.where(lane_of == c, jnp.where(even, from_even, from_odd), large)
     for k in range(8):
         row = jnp.where(meta_recv[k, 0:1, :] < LARGE_IDS, large[k:k + 1], small_best[k:k + 1, :])
@@ -487,55 +594,7 @@
 
     lax.fori_loop(1, 8, final_step, 0)
 
-    def drain_line(k, carry):
-        for copy in x_copies(k):
-            copy.wait_send()
-        final_copy(k).wait_send()
-        return carry
-
-    lax.fori_loop(1, 8, drain_line, 0)
-
-    def drain_plane(k, carry):
-        _, a, _ = axes(k)
-
-        def piece(step, inner):
-            for copy in first_copies(k, lax.rem(a + step, 4)):
-                copy.wait_send()
-            return inner
-
-        lax.fori_loop(1, 4, piece, 0)
-        split, stays = second_kind(k)
-
-        @pl.when(split)
-        def _():
-            for n in range(2):
-                for copy in split_copies(k, n):
-                    copy.wait_send()
-
-        @pl.when(jnp.logical_not(split | stays))
-        def _():
-            for copy in block_copies(k)[:2]:
-                copy.wait_send()
-
-        @pl.when(jnp.logical_not(busy))
-        def _():
-            for copy in turned_copies(k):
-                copy.wait_send()
-
-        return carry
-
-    lax.fori_loop(0, 8, drain_plane, 0)
-
-    @pl.when(busy)
-    def _():
-        def drain_share(k, carry):
-            for copy in share_copies(k):
-                copy.wait_send()
-            return carry
-
-        lax.fori_loop(0, 8, drain_share, 0)
-        for i in range(16):
-            pl.when(jnp.logical_not((b == i) & (host == core)))(result_copies(i)[0].wait_send)
+    lax.fori_loop(1, 8, lambda k, carry: (final_copy(k).wait_send(), carry)[1], 0)
 
 
 def shards(embeddings, cluster_ids, orders):
@@ -575,6 +634,7 @@
             dma((8,)), dma((8,)), dma((8,)), dma((8,)),
             dma((16,)), dma((8,)),
             dma((8,)), dma((8,)),
+            pltpu.SemaphoreType.REGULAR,
         ],
         compiler_params=pltpu.CompilerParams(
             collective_id=0, has_side_effects=True, vmem_limit_bytes=60 * 1024 * 1024),

time: 61.8 us -> 56.4 us (0.913)
  Pallas kernels: 60.3 us -> 54.9 us
    pallas_call x1, Pallas kernels: 60.3 us -> 54.9 us  [shards(): pl.pallas_call(kernel, out_shape=jax.ShapeDtypeStruct((8, SLOT), F32), in...]
where the time goes in v3:
time: 56.4 us; the launch traced here: 56.2 us
  Pallas kernels  54.9 us (97%)
  local copies, waits for them, and re-layouts  1.28 us (2%)
    pallas_call x1, Pallas kernels, shards(): pl.pallas_call(kernel, out_shape=jax.ShapeDtypeStruct((8, SLOT), F32), in...  54.9 us
    unnamed x1, local copies, waits for them, and re-layouts  1.28 us

profile of v3, /device:TPU:1, one launch (start us, length us, event | category | flops | bytes accessed | tf_op | source)
XLA Modules:
  0.0 56.2 jit_solution(122236802289859945)
XLA Ops:
  0.0 54.9 %shard_map.37 = f32[8,128]{1,0:T(8,128)} custom-call(bf16[8,128,768]{2,1,0:T(8,128)(2,1)} %bitcast.4, s32[8,128]{1,0:T(8,128)} %bitcast.6, s32[8,128]{1,0:T(8,128)} %bitcast.7), custom_call_target="tpu_custom_call" | custom-call | tf_op jit(solution)/shard_map/pallas_call | solution.py:603
  55.0 1.3 %copy.5 = f32[1,1,8,128]{3,2,1,0:T(8,128)} copy(f32[1,1,8,128]{3,2,1,0:T(8,128)} %bitcast.5) | data formatting | bytes 8192

commit v4 on v3

--- a/solution.py
+++ b/solution.py
@@ -13,7 +13,7 @@
 CAP = 32
 LARGE_IDS = 32.0
 NEVER = 1.0e9
-EARLY = 5
+EARLY = 4
 LAG = 4
 PASS = 2
 ORDER = sum(way << (3 * step) for step, way in enumerate((0, 1, 2, 6, 3, 7, 4, 5)))
@@ -475,7 +475,9 @@
             small_best[pl.ds(2 * q + i, 1), :] = to_row(column[i * SLOT:(i + 1) * SLOT])
         return carry
 
-    lax.fori_loop(0, 4, small, 0)
+    @pl.when(jnp.logical_not(busy))
+    def _():
+        lax.fori_loop(0, 4, small, 0)
 
     def result_copies(i):
         spot = 2 * z + core
@@ -489,10 +491,8 @@
 
     @pl.when(busy)
     def _():
-        if LAG > 2:
-            lax.fori_loop(8 - LAG, 6, lambda k, carry: (take(k), carry)[1], 0)
-        take(6)
-        take(7)
+        for k in range(8 - LAG, 8):
+            take(k)
         compare_same(7)
         for i in range(16):
             tile_send[i] = jnp.where(even, best[i % 4], best[i // 4])
@@ -500,6 +500,7 @@
             mine = (b == i) & (host == core)
             pl.when(jnp.logical_not(mine))(far.start)
             pl.when(mine)(near.start)
+        lax.fori_loop(0, 4, small, 0)
 
     def drain_line(k, carry):
         for copy in x_copies(k):

time: 56.4 us -> 53.5 us (0.949)
  Pallas kernels: 54.9 us -> 52 us
    pallas_call x1, Pallas kernels: 54.9 us -> 52 us  [shards(): pl.pallas_call(kernel, out_shape=jax.ShapeDtypeStruct((8, SLOT), F32), in...]
where the time goes in v4:
time: 53.5 us; the launch traced here: 53.3 us
  Pallas kernels  52 us (97%)
  local copies, waits for them, and re-layouts  1.28 us (2%)
    pallas_call x1, Pallas kernels, shards(): pl.pallas_call(kernel, out_shape=jax.ShapeDtypeStruct((8, SLOT), F32), in...  52 us
    unnamed x1, local copies, waits for them, and re-layouts  1.28 us

profile of v4, /device:TPU:1, one launch (start us, length us, event | category | flops | bytes accessed | tf_op | source)
XLA Modules:
  0.0 53.3 jit_solution(4053217213355093615)
XLA Ops:
  0.0 52.0 %shard_map.37 = f32[8,128]{1,0:T(8,128)} custom-call(bf16[8,128,768]{2,1,0:T(8,128)(2,1)} %bitcast.4, s32[8,128]{1,0:T(8,128)} %bitcast.6, s32[8,128]{1,0:T(8,128)} %bitcast.7), custom_call_target="tpu_custom_call" | custom-call | tf_op jit(solution)/shard_map/pallas_call | solution.py:604
  52.0 1.3 %copy.5 = f32[1,1,8,128]{3,2,1,0:T(8,128)} copy(f32[1,1,8,128]{3,2,1,0:T(8,128)} %bitcast.5) | data formatting | bytes 8192

commit v5 on v4

--- a/solution.py
+++ b/solution.py
@@ -14,9 +14,7 @@
 LARGE_IDS = 32.0
 NEVER = 1.0e9
 EARLY = 4
-LAG = 4
-PASS = 2
-ORDER = sum(way << (3 * step) for step, way in enumerate((0, 1, 2, 6, 3, 7, 4, 5)))
+ORDER = sum(way << (3 * step) for step, way in enumerate((0, 1, 6, 2, 7, 3, 4, 5)))
 
 
 def flip(value, bits):
@@ -94,7 +92,7 @@
     host = lax.div(offset, 2)
 
     def relation(k):
-        return lax.rem(lax.div(ORDER, lax.shift_left(1, 3 * k)), 8)
+        return lax.rem(lax.shift_right_logical(ORDER, 3 * k), 8)
 
     def partner(k):
         return flip(g, relation(k))
@@ -410,11 +408,8 @@
 
     def take(k):
         share(k)
-        if not isinstance(k, int):
-            pl.when(k >= 1)(lambda: compare_same(k - 1))
-        elif k >= 1:
-            compare_same(k - 1)
         compare_old(k)
+        compare_same(k)
 
     best[...] = jnp.full(best.shape, -1.0, F32)
     for copy in info:
@@ -434,6 +429,11 @@
         for copy in x_copies(k):
             copy.start()
         return carry
+
+    def arrive(k):
+        for copy in x_copies(k):
+            copy.wait_recv()
+        send_first(k)
 
     lax.fori_loop(1, EARLY, prepare_step, 0)
     pl.semaphore_wait(barrier, 19)
@@ -441,23 +441,28 @@
         pl.semaphore_signal(ready, inc=1, device_id=(4 * lax.rem(z + step, 4) + y, g), device_id_type=MESH)
     lax.fori_loop(1, EARLY, leave_step, 0)
     send_first(0)
+    pl.semaphore_wait(ready, 3)
+    arrive(1)
     lax.fori_loop(EARLY, 8, lambda k, carry: leave_step(k, prepare_step(k, carry)), 0)
-    pl.semaphore_wait(ready, 3)
-
-    def pass_on(k, carry):
-        for copy in x_copies(k):
-            copy.wait_recv()
-        send_first(k)
-        pl.when(k >= PASS)(lambda: send_second(k - PASS))
-
-        @pl.when(busy & (k >= LAG))
-        def _():
-            take(k - LAG)
-
-        return carry
-
-    lax.fori_loop(1, 8, pass_on, 0)
-    lax.fori_loop(8 - PASS, 8, lambda k, carry: (send_second(k), carry)[1], 0)
+
+    arrive(2)
+    send_second(0)
+    arrive(3)
+    send_second(1)
+    arrive(4)
+    send_second(2)
+    pl.when(busy)(lambda: take(0))
+    arrive(5)
+    send_second(3)
+    pl.when(busy)(lambda: take(1))
+    arrive(6)
+    send_second(4)
+    pl.when(busy)(lambda: take(2))
+    arrive(7)
+    send_second(5)
+    pl.when(busy)(lambda: take(3))
+    send_second(6)
+    send_second(7)
 
     def small(q, carry):
         query = recv[pl.ds(pl.multiple_of(q * 256, 256), 256)]
@@ -491,9 +496,8 @@
 
     @pl.when(busy)
     def _():
-        for k in range(8 - LAG, 8):
+        for k in range(4, 8):
             take(k)
-        compare_same(7)
         for i in range(16):
             tile_send[i] = jnp.where(even, best[i % 4], best[i // 4])
             far, near = result_copies(i)
@@ -501,62 +505,6 @@
             pl.when(jnp.logical_not(mine))(far.start)
             pl.when(mine)(near.start)
         lax.fori_loop(0, 4, small, 0)
-
-    def drain_line(k, carry):
-        for copy in x_copies(k):
-            copy.wait_send()
-        return carry
-
-    lax.fori_loop(1, 8, drain_line, 0)
-
-    def drain_plane(k, carry):
-        staged, a, _ = axes(k)
-
-        def piece(step, inner):
-            t = lax.rem(a + step, 4)
-            for copy in first_copies(k, t):
-                copy.wait_send()
-            return inner
-
-        lax.fori_loop(1, 4, piece, 0)
-
-        @pl.when(jnp.logical_not(staged | direct_near(a)))
-        def _():
-            for copy in direct_copies(k, a)[:2]:
-                copy.wait_send()
-
-        split, stays = second_kind(k)
-
-        @pl.when(staged & split)
-        def _():
-            for n in range(2):
-                for copy in split_copies(k, n):
-                    copy.wait_send()
-
-        @pl.when(staged & jnp.logical_not(split | stays))
-        def _():
-            for copy in block_copies(k)[:2]:
-                copy.wait_send()
-
-        @pl.when(jnp.logical_not(busy))
-        def _():
-            for copy in turned_copies(k):
-                copy.wait_send()
-
-        return carry
-
-    lax.fori_loop(0, 8, drain_plane, 0)
-
-    @pl.when(busy)
-    def _():
-        def drain_share(k, carry):
-            for copy in share_copies(k):
-                copy.wait_send()
-            return carry
-
-        lax.fori_loop(0, 8, drain_share, 0)
-        for i in range(16):
-            pl.when(jnp.logical_not((b == i) & (host == core)))(result_copies(i)[0].wait_send)
 
     lane_of = lax.div(iota((8, SLOT), 1), CAP)
     large = jnp.full((8, SLOT), -1.0, F32)
@@ -580,6 +528,62 @@
         return carry
 
     lax.fori_loop(1, 8, final_start, 0)
+    def drain_line(k, carry):
+        for copy in x_copies(k):
+            copy.wait_send()
+        return carry
+
+    lax.fori_loop(1, 8, drain_line, 0)
+
+    def drain_plane(k, carry):
+        staged, a, _ = axes(k)
+
+        def piece(step, inner):
+            t = lax.rem(a + step, 4)
+            for copy in first_copies(k, t):
+                copy.wait_send()
+            return inner
+
+        lax.fori_loop(1, 4, piece, 0)
+
+        @pl.when(jnp.logical_not(staged | direct_near(a)))
+        def _():
+            for copy in direct_copies(k, a)[:2]:
+                copy.wait_send()
+
+        split, stays = second_kind(k)
+
+        @pl.when(staged & split)
+        def _():
+            for n in range(2):
+                for copy in split_copies(k, n):
+                    copy.wait_send()
+
+        @pl.when(staged & jnp.logical_not(split | stays))
+        def _():
+            for copy in block_copies(k)[:2]:
+                copy.wait_send()
+
+        @pl.when(jnp.logical_not(busy))
+        def _():
+            for copy in turned_copies(k):
+                copy.wait_send()
+
+        return carry
+
+    lax.fori_loop(0, 8, drain_plane, 0)
+
+    @pl.when(busy)
+    def _():
+        def drain_share(k, carry):
+            for copy in share_copies(k):
+                copy.wait_send()
+            return carry
+
+        lax.fori_loop(0, 8, drain_share, 0)
+        for i in range(16):
+            pl.when(jnp.logical_not((b == i) & (host == core)))(result_copies(i)[0].wait_send)
+
     final_recv[0] = final_send[0]
 
     def unpermute(k):

time: 53.5 us -> 52.9 us (0.989)
    pallas_call x1, Pallas kernels: 52 us -> 51.5 us  [shards(): pl.pallas_call(kernel, out_shape=jax.ShapeDtypeStruct((8, SLOT), F32), in...]
where the time goes in v5:
time: 52.9 us; the launch traced here: 52.7 us
  Pallas kernels  51.5 us (97%)
  local copies, waits for them, and re-layouts  1.28 us (2%)
    pallas_call x1, Pallas kernels, shards(): pl.pallas_call(kernel, out_shape=jax.ShapeDtypeStruct((8, SLOT), F32), in...  51.5 us
    unnamed x1, local copies, waits for them, and re-layouts  1.28 us

profile of v5, /device:TPU:1, one launch (start us, length us, event | category | flops | bytes accessed | tf_op | source)
XLA Modules:
  0.0 52.7 jit_solution(12405182764543714832)
XLA Ops:
  0.0 51.5 %shard_map.37 = f32[8,128]{1,0:T(8,128)} custom-call(bf16[8,128,768]{2,1,0:T(8,128)(2,1)} %bitcast.4, s32[8,128]{1,0:T(8,128)} %bitcast.6, s32[8,128]{1,0:T(8,128)} %bitcast.7), custom_call_target="tpu_custom_call" | custom-call | tf_op jit(solution)/shard_map/pallas_call | solution.py:608
  51.5 1.3 %copy.5 = f32[1,1,8,128]{3,2,1,0:T(8,128)} copy(f32[1,1,8,128]{3,2,1,0:T(8,128)} %bitcast.5) | data formatting | bytes 8192

commit v6 on v5

--- a/solution.py
+++ b/solution.py
@@ -13,7 +13,7 @@
 CAP = 32
 LARGE_IDS = 32.0
 NEVER = 1.0e9
-EARLY = 4
+EARLY = 5
 ORDER = sum(way << (3 * step) for step, way in enumerate((0, 1, 6, 2, 7, 3, 4, 5)))
 
 
@@ -460,8 +460,8 @@
     pl.when(busy)(lambda: take(2))
     arrive(7)
     send_second(5)
+    send_second(6)
     pl.when(busy)(lambda: take(3))
-    send_second(6)
     send_second(7)
 
     def small(q, carry):

time: 52.9 us -> 53.7 us (1.015)
  Pallas kernels: 51.5 us -> 52.3 us
    pallas_call x1, Pallas kernels: 51.5 us -> 52.3 us  [shards(): pl.pallas_call(kernel, out_shape=jax.ShapeDtypeStruct((8, SLOT), F32), in...]
where the time goes in v6:
time: 53.7 us; the launch traced here: 53.5 us
  Pallas kernels  52.3 us (97%)
  local copies, waits for them, and re-layouts  1.28 us (2%)
    pallas_call x1, Pallas kernels, shards(): pl.pallas_call(kernel, out_shape=jax.ShapeDtypeStruct((8, SLOT), F32), in...  52.3 us
    unnamed x1, local copies, waits for them, and re-layouts  1.28 us

profile of v6, /device:TPU:1, one launch (start us, length us, event | category | flops | bytes accessed | tf_op | source)
XLA Modules:
  0.0 53.5 jit_solution(13742374540154313125)
XLA Ops:
  0.0 52.3 %shard_map.37 = f32[8,128]{1,0:T(8,128)} custom-call(bf16[8,128,768]{2,1,0:T(8,128)(2,1)} %bitcast.4, s32[8,128]{1,0:T(8,128)} %bitcast.6, s32[8,128]{1,0:T(8,128)} %bitcast.7), custom_call_target="tpu_custom_call" | custom-call | tf_op jit(solution)/shard_map/pallas_call | solution.py:608
  52.3 1.3 %copy.5 = f32[1,1,8,128]{3,2,1,0:T(8,128)} copy(f32[1,1,8,128]{3,2,1,0:T(8,128)} %bitcast.5) | data formatting | bytes 8192
